TPU v7x, 256 devices: a whole 4x4x8 slice. The times are simulated.
256 devices in a mesh: grp: 4 (over z_lo, core), seq: 16 (over y, z_hi), tile: 4 (over x).
Axes of the slice: x: 4, y: 4, z: 8 (z_hi: 4, z_lo: 2; z = z_hi * 2 + z_lo), core: 2. Of those that a mesh axis runs over, the one named last changes fastest.
Arguments:
- base_q: bfloat16 [4, 32, 32, 3072], P('grp', 'seq', None, 'tile'), may hold values from -20 to 20
- base_k: bfloat16 [4, 32, 32, 3072], P('grp', 'seq', None, 'tile'), may hold values from -20 to 20
- base_v: bfloat16 [4, 32, 32, 3072], P('grp', 'seq', None, 'tile'), may hold values from -6 to 6
- frame_stretch: int32 [4], replicated, may hold values from 0 to 1, never falling along the last dimension, each value on 1 to 3 neighbouring positions
- bridge_w: bfloat16 [3072, 1536], P('tile'), may hold values from -0.109375 to 0.109375
- sr_latent: bfloat16 [4, 64, 64, 1536], P(None, 'seq', 'tile'), may hold values from -6 to 6
- sr_wq: bfloat16 [1536, 1536], P(None, 'grp'), may hold values from -3 to 3
- sr_wk: bfloat16 [1536, 1536], P(None, 'grp'), may hold values from -3 to 3
- sr_wv: bfloat16 [1536, 1536], P(None, 'grp'), may hold values from -0.15625 to 0.15625
Outputs:
- sr_out: bfloat16 [4, 64, 64, 1536], P(None, 'seq', 'tile', 'grp')
All inputs are finite; a program needn't handle non-finite values.
Results may differ from a plain program's by a relative error of at most 0.033.
Values may be sent and summed in bfloat16 or wider, within the bound.
A program may use at most 128 MiB of HBM per device.

v0:
```python
import math

import jax
import jax.numpy as jnp
from jax import lax
from jax.sharding import PartitionSpec as P

HEAD = 128
RAD = 2


def extended(shard, sides, width):
    for axis, dim in sides:
        peers, length = (lax.axis_size(axis), shard.shape[dim])
        up = [(i, (i + 1) % peers) for i in range(peers - 1)]
        down = [(j, i) for i, j in up]
        last = lax.slice_in_dim(shard, length - width, length, axis=dim)
        initial = lax.slice_in_dim(shard, 0, width, axis=dim)
        before = lax.ppermute(last, axis, up)
        after = lax.ppermute(initial, axis, down)
        shard = jnp.concatenate([before, shard, after], axis=dim)
    return shard


def stretch_lookup(frame_ids, frame_stretch):
    matches = frame_ids[:, None] == jnp.arange(frame_stretch.shape[0], dtype=jnp.int32)[None, :]
    return jnp.sum(jnp.where(matches, frame_stretch[None, :], 0), axis=1)


def local(base_q, base_k, base_v, frame_stretch, bridge_w, sr_latent, sr_wq, sr_wk, sr_wv):
    group_count = lax.axis_size("grp")
    tile_count = lax.axis_size("tile")
    seq_count = lax.axis_size("seq")
    frames_local, rows_local, row_cells, columns = base_q.shape
    heads_local = columns // HEAD
    all_frames = frames_local * group_count
    token_count = frames_local * rows_local * row_cells
    score_scale = HEAD ** (-0.5)
    sr_width = bridge_w.shape[1]
    queries = base_q.reshape(token_count, heads_local, HEAD)
    query_frame = lax.axis_index("grp") * frames_local + jnp.arange(
        token_count, dtype=jnp.int32
    ) // (rows_local * row_cells)
    query_groups = 1
    query_stretch = stretch_lookup(query_frame, frame_stretch)
    group_rows = queries.shape[0] // query_groups
    query_parts = [queries]
    stretch_parts = [query_stretch]
    stretch_tops = [jnp.max(piece_stretch) for piece_stretch in stretch_parts]

    def absorb(state, key_block, value_block, block_stretch, query_part, stretch_part):
        running_top, running_total, running_sum = state
        scores = (
            jnp.einsum("qhd,khd->hqk", query_part, key_block, preferred_element_type=jnp.float32)
            * score_scale
        )
        visible = block_stretch[None, None, :] <= stretch_part[None, :, None]
        block_top = jnp.max(jnp.where(visible, scores, -1e30), axis=-1)
        new_top = jnp.maximum(running_top, block_top)
        carried = jnp.exp(running_top - new_top)
        unscaled = jnp.where(visible, jnp.exp(scores - new_top[..., None]), 0.0)
        new_total = running_total * carried + jnp.sum(unscaled, axis=-1)
        new_sum = running_sum * carried[..., None] + jnp.einsum(
            "hqk,khd->hqd",
            unscaled.astype(jnp.bfloat16),
            value_block,
            preferred_element_type=jnp.float32,
        )
        return (new_top, new_total, new_sum)

    initial = tuple(
        (
            (
                jnp.full((heads_local, group_rows), -1e30, jnp.float32),
                jnp.zeros((heads_local, group_rows), jnp.float32),
                jnp.zeros((heads_local, group_rows, HEAD), jnp.float32),
            )
            for part in range(query_groups)
        )
    )
    key_flat = base_k.reshape(token_count, heads_local, HEAD)
    value_flat = base_v.reshape(token_count, heads_local, HEAD)
    carry = initial
    key_piece = lax.all_gather(key_flat, ("grp", "seq"), axis=0, tiled=True)
    value_piece = lax.all_gather(value_flat, ("grp", "seq"), axis=0, tiled=True)
    piece_rows = key_piece.shape[0]
    block_rows = math.gcd(piece_rows, 1024)
    block_count = piece_rows // block_rows
    key_index = jnp.arange(piece_rows, dtype=jnp.int32)
    source = key_index // token_count
    key_frame = source // seq_count * frames_local + key_index % token_count // (
        rows_local * row_cells
    )
    key_stretch = stretch_lookup(key_frame, frame_stretch)
    blocks = (
        key_piece.reshape(block_count, block_rows, heads_local, HEAD),
        value_piece.reshape(block_count, block_rows, heads_local, HEAD),
        key_stretch.reshape(block_count, block_rows),
    )

    def scan_step(states, inputs):
        key_block, value_block, block_stretch = inputs
        lowest = jnp.min(block_stretch)
        part = 0

        def refresh(state, part=part):
            return absorb(
                state, key_block, value_block, block_stretch, query_parts[part], stretch_parts[part]
            )

        def unchanged(state):
            return state

        updated = [lax.cond(lowest <= stretch_tops[part], refresh, unchanged, states[part])]
        return (tuple(updated), None)

    carry, unused = lax.scan(scan_step, carry, blocks)
    states = carry
    outputs = [(state[2] / state[1][..., None]).astype(jnp.bfloat16) for state in states]
    attended = outputs[0].transpose(1, 0, 2).reshape(-1, columns)
    partial_value = jnp.dot(attended, bridge_w, preferred_element_type=jnp.float32)
    partial_value = partial_value.reshape(frames_local, rows_local, row_cells, sr_width)
    summed = lax.psum_scatter(
        partial_value.astype(jnp.bfloat16), "tile", scatter_dimension=2, tiled=True
    ).astype(jnp.float32)
    condition = summed * lax.rsqrt(jnp.mean(summed * summed, axis=-1, keepdims=True) + 1e-06)
    collected = lax.all_gather(
        condition[None].astype(jnp.bfloat16), "grp", axis=0, tiled=True
    ).astype(jnp.float32)
    condition = collected.reshape(all_frames, rows_local, -1, sr_width)
    upsampled = jnp.repeat(jnp.repeat(condition, 2, axis=1), 2, axis=2)
    hidden = sr_latent.astype(jnp.float32) + upsampled
    normed = (hidden * lax.rsqrt(jnp.mean(hidden * hidden, axis=-1, keepdims=True) + 1e-06)).astype(
        jnp.bfloat16
    )
    sr_rows = sr_latent.shape[1]
    sr_cols = sr_latent.shape[2]
    flat_cells = normed.reshape(-1, sr_width)
    head_cols = sr_wq.shape[1]
    sr_heads = head_cols // HEAD
    sr_query = jnp.dot(flat_cells, sr_wq, preferred_element_type=jnp.float32).astype(jnp.bfloat16)
    sr_key = jnp.dot(flat_cells, sr_wk, preferred_element_type=jnp.float32).astype(jnp.bfloat16)
    sr_value = jnp.dot(flat_cells, sr_wv, preferred_element_type=jnp.float32).astype(jnp.bfloat16)
    packed = jnp.concatenate([sr_key, sr_value], axis=-1).reshape(
        all_frames, sr_rows, sr_cols, 2 * head_cols
    )
    padded = extended(packed, (("seq", 1), ("tile", 2)), RAD)
    row_global = (
        lax.axis_index("seq") * sr_rows - RAD + jnp.arange(sr_rows + 2 * RAD, dtype=jnp.int32)
    )
    row_inside = (row_global >= 0) & (row_global < sr_rows * seq_count)
    col_global = (
        lax.axis_index("tile") * sr_cols - RAD + jnp.arange(sr_cols + 2 * RAD, dtype=jnp.int32)
    )
    col_inside = (col_global >= 0) & (col_global < sr_cols * tile_count)
    inside = row_inside[:, None] & col_inside[None, :]
    query_cells = sr_query.reshape(all_frames, sr_rows, sr_cols, sr_heads, HEAD)
    span = 2 * RAD + 1
    score_list = []
    mask_list = []
    for row_step in range(span):
        for col_step in range(span):
            window = padded[
                :, row_step : row_step + sr_rows, col_step : col_step + sr_cols, :head_cols
            ]
            key_window = window.reshape(all_frames, sr_rows, sr_cols, sr_heads, HEAD)
            score_list.append(
                jnp.einsum(
                    "fijhd,fijhd->fijh", query_cells, key_window, preferred_element_type=jnp.float32
                )
                * score_scale
            )
            mask_list.append(
                inside[row_step : row_step + sr_rows, col_step : col_step + sr_cols][
                    None, :, :, None
                ]
            )
    scores = jnp.stack(score_list)
    allowed = jnp.broadcast_to(jnp.stack(mask_list), scores.shape)
    row_top = jnp.max(jnp.where(allowed, scores, -jnp.inf), axis=0)
    unscaled = jnp.where(allowed, jnp.exp(scores - row_top), 0.0)
    weights = (unscaled / jnp.sum(unscaled, axis=0)).astype(jnp.bfloat16)
    blended = jnp.zeros((all_frames, sr_rows, sr_cols, sr_heads, HEAD), jnp.float32)
    for row_step in range(span):
        for col_step in range(span):
            position = row_step * span + col_step
            window = padded[
                :, row_step : row_step + sr_rows, col_step : col_step + sr_cols, head_cols:
            ]
            value_window = window.reshape(all_frames, sr_rows, sr_cols, sr_heads, HEAD).astype(
                jnp.float32
            )
            blended = blended + weights[position].astype(jnp.float32)[..., None] * value_window
    return blended.reshape(all_frames, sr_rows, sr_cols, head_cols).astype(jnp.bfloat16)


def solution(mesh):
    placed = (
        P("grp", "seq", None, "tile"),
        P("grp", "seq", None, "tile"),
        P("grp", "seq", None, "tile"),
        P(),
        P("tile", None),
        P(None, "seq", "tile", None),
        P(None, "grp"),
        P(None, "grp"),
        P(None, "grp"),
    )
    return jax.shard_map(
        local, mesh=mesh, in_specs=placed, out_specs=P(None, "seq", "tile", "grp"), check_vma=False
    )
```

profile of v0, /device:TPU:6, one launch (start us, length us, event | category | flops | bytes accessed | tf_op | source)
XLA Modules:
  0.0 609.4 jit_solution(6684401876481214026)
XLA Ops:
  6.5 1.2 reshape.503
  8.5 1.0 reshape.506
  10.2 1.0 reshape.505
  13.8 189.6 %all-gather.4.cloned.1.call-done = bf16[4096,6,128]{2,0,1:T(8,128)(2,1)} async-done(((bf16[64,6,128]{2,0,1:T(8,128)(2,1)}), bf16[4096,6,128]{2,0,1:T(8,128)(2,1)}) %all-gather.4.cloned.1.call-update) | async-done | bytes 6291472 | tf_op jit(solution)/shard_map/all_gather | solution.py:84
  203.5 6.0 copy.2540
  209.5 189.0 %all-gather.6.cloned.1.call-done = bf16[4096,6,128]{2,0,1:T(8,128)(2,1)} async-done(((bf16[64,6,128]{2,0,1:T(8,128)(2,1)}), bf16[4096,6,128]{2,0,1:T(8,128)(2,1)}) %all-gather.6.cloned.1.call-update) | async-done | bytes 6291472 | tf_op jit(solution)/shard_map/all_gather | solution.py:85
  398.5 6.0 copy.2542
  404.6 12.8 %while.14 = (s32[]{:T(128)}, f32[6,64]{1,0:T(8,128)S(1)}, f32[6,64]{1,0:T(8,128)S(1)}, f32[6,64,128]{2,1,0:T(8,128)S(1)}, s32[4,1024]{1,0:T(4,128)S(1)}, /*index...) while((s32[]{:T(128)}, f32[6,64]{1,0:T(8,128)S(1)}, ...), condition=%wide.region_9.10_spmd, body=%wide.region_3.9_spmd.sunk | while | flops 205031168 | bytes 8656387 | solution.py:117
  406.6 4.7 conditional.2
  406.7 2.2 fusion.2
  409.4 1.9 fusion.14
  419.4 37.0 %reduce-scatter.4.cloned.1.call-done = bf16[8,3072]{1,0:T(8,128)(2,1)} async-done(((bf16[32,3072]{1,0:T(8,128)(2,1)}), bf16[8,3072]{1,0:T(8,128)(2,1)}) %reduce-scatter.4.cloned.1.call-update) | async-done | bytes 49168
  457.4 5.6 all-gather
  463.6 1.1 reshape.511
  464.7 1.5 multiply_reduce_fusion
  466.5 1.0 copy-done.46
  468.8 4.4 collective-permute-start
  473.2 1.3 collective-permute-start.1
  475.2 3.7 collective-permute-done
  478.9 9.4 %collective-permute-done.1 = bf16[4,2,16,768]{3,2,1,0:T(8,128)(2,1)S(1)} collective-permute-done((bf16[4,2,16,768]{3,2,1,0:T(8,128)(2,1)S(1)}, bf16[4,2,16,768]{3,2,1,0:T(8,128)(2,1)S(1)}, u32[]{:S(2)}, u32[]{:S(2)}) %collective-permute-start.1) | collective-permute-done | bytes 196640 | tf_op jit(solution)/shard_map/ppermute | solution.py:20
  488.4 1.3 collective-permute-start.2
  489.7 5.6 collective-permute-start.3
  499.3 1.5 maximum_maximum_fusion
  500.8 1.4 fusion.112
  502.4 1.4 fusion.113
  503.8 1.0 reshape.534
  504.8 1.0 reshape.535
  505.8 1.0 reshape.536
  506.8 1.0 reshape.538
  507.8 2.7 fusion.55
  511.9 1.7 broadcast_multiply_fusion.3
  516.0 1.0 reshape.519
  520.1 1.8 reshape.525
  521.8 1.7 reshape.526
  523.5 1.7 reshape.528
  525.2 1.7 reshape.529
  526.9 1.7 reshape.530
  528.6 1.7 reshape.531
  530.3 1.7 reshape.539
  532.0 8.0 %fusion.56 = (f32[4,4,16,3]{3,2,1,0:T(8,128)S(1)}, f32[4,4,16,3]{3,2,1,0:T(8,128)S(1)}, f32[4,4,16,3]{3,2,1,0:T(8,128)S(1)}, f32[4,4,16,3]{3,2,1,0:T(8,128)}, f3...) fusion(bf16[4,4,16,3,128]{4,3,2,1,0:T(4,128)(2,1)S(1)} %reshape, ...), kind=kLoop, calls=%fused_computation.101 | loop fusion | flops 5392896 | bytes 3790848
  540.8 1.0 broadcast_multiply_fusion.8
  542.6 1.0 broadcast_multiply_fusion.10
  550.9 1.7 copy.2726
  558.4 1.0 mul.437
  559.9 1.0 mul.458
  561.4 1.0 mul.461
  562.9 1.0 mul.464
  564.3 1.0 mul.467
  565.8 1.0 mul.470
  567.3 1.0 mul.473
  568.8 1.0 mul.476
  570.2 1.0 mul.479
  571.7 1.0 mul.482
  573.2 1.0 mul.485
  574.7 1.0 mul.488
  579.1 1.0 mul.497
  580.6 1.0 mul.500
  582.2 1.0 mul.503
  583.7 1.0 mul.506
  586.6 1.0 mul.440
  589.6 1.0 mul.446
  592.5 1.0 mul.452
  594.1 1.0 mul.455
  595.0 7.6 %add_convert_fusion = bf16[4,4,16,384]{3,2,1,0:T(8,128)(2,1)} fusion(f32[4,4,16,384]{3,2,1,0:T(8,128)} %mul.509, f32[4,4,16,384]{3,2,1,0:T(8,128)} %mul.506, f32[4,4,16,384]{3,2,1,0:T(8,128)} %mul.503, f32[4,4,16,384]{3,2,1,0:T(8,128)} %mul.500, f32[4,4,16,384]{3,2,1,0:T(8,128)} %mul.497, f32[4,4,16,384]{3,2,1,0:T(8,128)} %mul.494, ...), kind=kLoop, calls=%fused_computation.104 | loop fusion | flops 8552448 | bytes 14942208 | tf_op jit(solution)/shard_map/convert_element_type | solution.py:194
  (311 shorter events, 55.3 us)
Async XLA Ops:
  6.5 411.2 %copy-start = (bf16[768,1536]{1,0:T(8,128)(2,1)S(1)}, bf16[768,1536]{1,0:T(8,128)(2,1)}, u32[]{:S(2)}) copy-start(bf16[768,1536]{1,0:T(8,128)(2,1)} %param.17) | copy-start | bytes 7077892
  6.5 4.7 copy-start.45
  6.5 196.9 %all-gather.4.cloned.1.call-start = ((), (), s32[]{:S(2)}) async-start(), calls=%async_computation.1 | async-start | bytes 6389760 | tf_op jit(solution)/shard_map/all_gather | solution.py:84
  8.4 390.1 %all-gather.6.cloned.1.call-start = ((), (), s32[]{:S(2)}) async-start(), calls=%async_computation.2 | async-start | bytes 6389760 | tf_op jit(solution)/shard_map/all_gather | solution.py:85
  10.2 446.2 %reduce-scatter.4.cloned.1.call-start = ((), (), s32[]{:S(2)}) async-start(), calls=%async_computation.3 | async-start | bytes 245760
  464.7 1.5 copy-start.6
  466.2 1.3 copy-start.46
  466.5 1.6 copy-start.47
  468.1 6.4 %copy-start.48 = (bf16[1536,384]{1,0:T(8,128)(2,1)S(1)}, bf16[1536,384]{1,0:T(8,128)(2,1)}, u32[]{:S(2)}) copy-start(bf16[1536,384]{1,0:T(8,128)(2,1)} %param.19) | copy-start | bytes 3538948
  468.7 30.5 %copy-start.3 = (bf16[256,768]{1,0:T(8,128)(2,1)}, bf16[256,768]{1,0:T(8,128)(2,1)S(1)}, u32[]{:S(2)}) copy-start(bf16[256,768]{1,0:T(8,128)(2,1)S(1)} %pad_maximum_fusion.1) | copy-start | bytes 1179652
  468.8 10.1 %collective-permute-start = (bf16[4,2,16,768]{3,2,1,0:T(8,128)(2,1)S(1)}, bf16[4,2,16,768]{3,2,1,0:T(8,128)(2,1)S(1)}, u32[]{:S(2)}, u32[]{:S(2)}) collective-permute-start(bf16[4,2,16,768]{3,2,1,0:T(8,128)(2,1)S(1)} %get-tuple-element.526), channel_id=1, source_target_pairs={{0,4},{4,8},{8,12},{12,16},{16,20},{20,24},{24,28},{28,32},{32,36}... | collective-permute-start | bytes 589832 | tf_op jit(solution)/shard_map/ppermute | solution.py:19
  473.2 15.0 %collective-permute-start.1 = (bf16[4,2,16,768]{3,2,1,0:T(8,128)(2,1)S(1)}, bf16[4,2,16,768]{3,2,1,0:T(8,128)(2,1)S(1)}, u32[]{:S(2)}, u32[]{:S(2)}) collective-permute-start(bf16[4,2,16,768]{3,2,1,0:T(8,128)(2,1)S(1)} %get-tuple-element.527), channel_id=1, source_target_pairs={{4,0},{8,4},{12,8},{16,12},{20,16},{24,20},{28,24},{32,28},{36,32}... | collective-permute-start | bytes 589832 | tf_op jit(solution)/shard_map/ppermute | solution.py:20
  478.9 20.4 %copy-start.4 = (bf16[4,2,16,768]{3,2,1,0:T(8,128)(2,1)}, bf16[4,2,16,768]{3,2,1,0:T(8,128)(2,1)S(1)}, u32[]{:S(2)}) copy-start(bf16[4,2,16,768]{3,2,1,0:T(8,128)(2,1)S(1)} %collective-permute-done) | copy-start | bytes 589828
  488.2 11.0 %copy-start.5 = (bf16[4,2,16,768]{3,2,1,0:T(8,128)(2,1)}, bf16[4,2,16,768]{3,2,1,0:T(8,128)(2,1)S(1)}, u32[]{:S(2)}) copy-start(bf16[4,2,16,768]{3,2,1,0:T(8,128)(2,1)S(1)} %collective-permute-done.1) | copy-start | bytes 589828
  488.4 10.9 %collective-permute-start.2 = (bf16[4,8,2,768]{3,2,1,0:T(2,128)(2,1)S(1)}, bf16[4,8,2,768]{3,2,1,0:T(2,128)(2,1)S(1)}, u32[]{:S(2)}, u32[]{:S(2)}) collective-permute-start(bf16[4,8,2,768]{3,2,1,0:T(2,128)(2,1)S(1)} %get-tuple-element.517), channel_id=1, source_target_pairs={{0,1},{1,2},{2,3},{4,5},{5,6},{6,7},{8,9},{9,10},{10,11},{12,13},{... | collective-permute-start | bytes 294920 | tf_op jit(solution)/shard_map/ppermute | solution.py:19
  489.7 9.6 %collective-permute-start.3 = (bf16[4,8,2,768]{3,2,1,0:T(2,128)(2,1)S(1)}, bf16[4,8,2,768]{3,2,1,0:T(2,128)(2,1)}, u32[]{:S(2)}, u32[]{:S(2)}) collective-permute-start(bf16[4,8,2,768]{3,2,1,0:T(2,128)(2,1)S(1)} %get-tuple-element.518), channel_id=1, source_target_pairs={{1,0},{2,1},{3,2},{5,4},{6,5},{7,6},{9,8},{10,9},{11,10},{13,12},{... | collective-permute-start | bytes 294920 | tf_op jit(solution)/shard_map/ppermute | solution.py:20
  500.8 1.6 copy-start.2
  503.8 4.1 copy-start.11
  510.5 5.3 copy-start.14
  510.5 5.4 copy-start.17
  511.2 5.8 copy-start.13
  511.9 5.8 copy-start.12
  513.6 4.9 copy-start.16
  515.1 4.2 copy-start.15
  520.1 11.9 %copy-start.7 = (bf16[4,4,16,3,128]{4,3,2,1,0:T(4,128)(2,1)S(1)}, bf16[4,4,16,3,128]{4,3,2,1,0:T(4,128)(2,1)}, u32[]{:S(2)}) copy-start(bf16[4,4,16,3,128]{4,3,2,1,0:T(4,128)(2,1)} %reshape.517) | copy-start | bytes 589828
  520.1 11.9 %copy-start.8 = (bf16[4,4,16,3,128]{4,3,2,1,0:T(4,128)(2,1)S(1)}, bf16[4,4,16,3,128]{4,3,2,1,0:T(4,128)(2,1)}, u32[]{:S(2)}) copy-start(bf16[4,4,16,3,128]{4,3,2,1,0:T(4,128)(2,1)} %reshape.522) | copy-start | bytes 589828
  520.1 11.9 %copy-start.9 = (bf16[4,4,16,3,128]{4,3,2,1,0:T(4,128)(2,1)S(1)}, bf16[4,4,16,3,128]{4,3,2,1,0:T(4,128)(2,1)}, u32[]{:S(2)}) copy-start(bf16[4,4,16,3,128]{4,3,2,1,0:T(4,128)(2,1)} %reshape.527) | copy-start | bytes 589828
  520.1 11.9 %copy-start.10 = (bf16[4,4,16,3,128]{4,3,2,1,0:T(4,128)(2,1)S(1)}, bf16[4,4,16,3,128]{4,3,2,1,0:T(4,128)(2,1)}, u32[]{:S(2)}) copy-start(bf16[4,4,16,3,128]{4,3,2,1,0:T(4,128)(2,1)} %reshape.532) | copy-start | bytes 589828
  540.0 4.4 copy-start.26
  540.0 4.4 copy-start.27
  540.0 5.2 copy-start.24
  540.0 5.2 copy-start.25
  540.1 6.0 copy-start.22
  540.1 5.9 copy-start.23
  541.8 5.0 copy-start.20
  541.8 5.0 copy-start.21
  543.6 4.0 copy-start.18
  543.6 4.0 copy-start.19
  545.2 4.7 copy-start.28
  547.6 6.6 %copy-start.31 = (f32[4,4,16,3]{3,2,1,0:T(8,128)S(1)}, f32[4,4,16,3]{3,2,1,0:T(8,128)}, u32[]{:S(2)}) copy-start(f32[4,4,16,3]{3,2,1,0:T(8,128)} %get-tuple-element.557) | copy-start | bytes 9220
  547.6 6.7 %copy-start.30 = (f32[4,4,16,3]{3,2,1,0:T(8,128)S(1)}, f32[4,4,16,3]{3,2,1,0:T(8,128)}, u32[]{:S(2)}) copy-start(f32[4,4,16,3]{3,2,1,0:T(8,128)} %get-tuple-element.555) | copy-start | bytes 9220
  548.3 6.2 %copy-start.29 = (f32[4,4,16,3]{3,2,1,0:T(8,128)S(1)}, f32[4,4,16,3]{3,2,1,0:T(8,128)}, u32[]{:S(2)}) copy-start(f32[4,4,16,3]{3,2,1,0:T(8,128)} %get-tuple-element.553) | copy-start | bytes 9220
  549.1 7.3 %copy-start.41 = (f32[4,4,16,3]{2,1,3,0:T(4,128)S(1)}, f32[4,4,16,3]{2,1,3,0:T(4,128)}, u32[]{:S(2)}) copy-start(f32[4,4,16,3]{2,1,3,0:T(4,128)} %copy.2727) | copy-start | bytes 9220
  549.1 7.4 %copy-start.40 = (f32[4,4,16,3]{2,1,3,0:T(4,128)S(1)}, f32[4,4,16,3]{2,1,3,0:T(4,128)}, u32[]{:S(2)}) copy-start(f32[4,4,16,3]{2,1,3,0:T(4,128)} %copy.2729) | copy-start | bytes 9220
  549.1 7.4 %copy-start.39 = (f32[4,4,16,3]{2,1,3,0:T(4,128)S(1)}, f32[4,4,16,3]{2,1,3,0:T(4,128)}, u32[]{:S(2)}) copy-start(f32[4,4,16,3]{2,1,3,0:T(4,128)} %copy.2731) | copy-start | bytes 9220
  549.1 7.4 %copy-start.38 = (f32[4,4,16,3]{2,1,3,0:T(4,128)S(1)}, f32[4,4,16,3]{2,1,3,0:T(4,128)}, u32[]{:S(2)}) copy-start(f32[4,4,16,3]{2,1,3,0:T(4,128)} %copy.2733) | copy-start | bytes 9220
  549.1 7.5 %copy-start.37 = (f32[4,4,16,3]{2,1,3,0:T(4,128)S(1)}, f32[4,4,16,3]{2,1,3,0:T(4,128)}, u32[]{:S(2)}) copy-start(f32[4,4,16,3]{2,1,3,0:T(4,128)} %copy.2735) | copy-start | bytes 9220
  549.1 7.5 %copy-start.36 = (f32[4,4,16,3]{2,1,3,0:T(4,128)S(1)}, f32[4,4,16,3]{2,1,3,0:T(4,128)}, u32[]{:S(2)}) copy-start(f32[4,4,16,3]{2,1,3,0:T(4,128)} %copy.2737) | copy-start | bytes 9220
  549.9 6.8 %copy-start.35 = (f32[4,4,16,3]{2,1,3,0:T(4,128)S(1)}, f32[4,4,16,3]{2,1,3,0:T(4,128)}, u32[]{:S(2)}) copy-start(f32[4,4,16,3]{2,1,3,0:T(4,128)} %copy.2739) | copy-start | bytes 9220
  549.9 6.8 %copy-start.34 = (f32[4,4,16,3]{2,1,3,0:T(4,128)S(1)}, f32[4,4,16,3]{2,1,3,0:T(4,128)}, u32[]{:S(2)}) copy-start(f32[4,4,16,3]{2,1,3,0:T(4,128)} %copy.2740) | copy-start | bytes 9220
  549.9 6.8 %copy-start.33 = (f32[4,4,16,3]{2,1,3,0:T(4,128)S(1)}, f32[4,4,16,3]{2,1,3,0:T(4,128)}, u32[]{:S(2)}) copy-start(f32[4,4,16,3]{2,1,3,0:T(4,128)} %copy.2742) | copy-start | bytes 9220
  550.0 6.8 %copy-start.32 = (f32[4,4,16,3]{2,1,3,0:T(4,128)S(1)}, f32[4,4,16,3]{2,1,3,0:T(4,128)}, u32[]{:S(2)}) copy-start(f32[4,4,16,3]{2,1,3,0:T(4,128)} %copy.2744) | copy-start | bytes 9220
  550.9 5.5 copy-start.42
  553.3 3.1 copy-start.44
  553.3 3.1 copy-start.43
  595.0 7.6 %copy-start.1 = (bf16[768,1536]{1,0:T(8,128)(2,1)S(1)}, bf16[768,1536]{1,0:T(8,128)(2,1)}, u32[]{:S(2)}) copy-start(bf16[768,1536]{1,0:T(8,128)(2,1)} %param.17) | copy-start | bytes 7077892
Sparse Core Ops, SparseCore 0:
  9.2 194.2 all-gather.3
  205.3 193.1 all-gather.5
  419.3 36.9 reduce-scatter.3
where the time goes:
time: 617 us; the launch traced here: 609 us
  waiting for transfers between devices  429 us (70%)
  local copies, waits for them, and re-layouts  103 us (17%)
  other arithmetic  33.2 us (5%)
  between operations  14.5 us (2%)
  starting transfers between devices  12.7 us (2%)
  matrix products  6.38 us (1%)
    all_gather x1, waiting for transfers between devices, local(): key_piece = lax.all_gather(key_flat, ('grp', 'seq'), axis=0, tiled=True)  190 us
    all_gather x1, waiting for transfers between devices, local(): value_piece = lax.all_gather(value_flat, ('grp', 'seq'), axis=0, tiled=True)  189 us
    unnamed x4, waiting for transfers between devices  37.1 us
    mul x50, local copies, waits for them, and re-layouts, local(): weights[position].astype(jnp.float32)[..., None] * value_window  32.7 us
    reshape x25, local copies, waits for them, and re-layouts, local(): key_window = window.reshape(all_frames, sr_rows, sr_cols, sr_heads, HEAD)  24 us
    unnamed x174, local copies, waits for them, and re-layouts  20.4 us
  transfers between devices with their start and end apart: 7, of which 5 were waited for; matrix products, arithmetic and copies ran while one was open for 3% of the time, Pallas kernels for 0%

commit v1 on v0

v1 whole, which is shorter than its diff:
```python
import functools
import math

import jax
import jax.numpy as jnp
from jax import lax
from jax.experimental import pallas as pl
from jax.experimental.pallas import tpu as pltpu
from jax.sharding import PartitionSpec as P

HEAD = 128
HEADS_TILE = 6
EPS = 1e-06
LOW = -1e30
EXP2_SCALE = HEAD ** (-0.5) * math.log2(math.e)
MESH = pl.DeviceIdType.MESH
BF16 = jnp.bfloat16
F32 = jnp.float32
NT = (((1,), (1,)), ((), ()))


def iota(shape, dim):
    return lax.broadcasted_iota(jnp.int32, shape, dim)


def one_hot(mask):
    return jnp.where(mask, 1.0, 0.0).astype(BF16)


def dot(a, b):
    return jnp.dot(a, b, preferred_element_type=F32)


def kernel(
    q_hbm, k_hbm, v_hbm, stretch, wb_hbm, lat_hbm, wq_hbm, wk_hbm, wv_hbm, out_hbm,
    q_buf, k_buf, v_buf, m_ref, l_ref, acc_ref, o_buf, a_buf, wb, wq, wk, wv,
    lat, edge_out, edge_in, p_own, p_send, p_recv, cond, x_buf, sr_q, sr_k, sr_v, out_buf,
    first_send, first_recv, own_send, fwd_send, relay_send, second_recv, ret_send, ret_recv,
    tile_send, tile_recv, cond_send, cond_recv, row_send, row_recv, col_send, col_recv,
    load_sem, out_sem,
):
    g, s, t = (lax.axis_index(name) for name in ("grp", "seq", "tile"))
    zl, c = g // 2, g % 2
    y, zh = s // 4, s % 4
    z = zh * 2 + zl
    sib = zl * 2 + (1 - c)
    s_up, s_down = (s + 1) % 16, (s + 15) % 16

    def dev(grp, seq, tile=t):
        return {"grp": grp, "seq": seq, "tile": tile}

    def remote(src, dst, send, recv, to):
        return pltpu.make_async_remote_copy(
            src_ref=src, dst_ref=dst, send_sem=send, recv_sem=recv, device_id=to, device_id_type=MESH
        )

    def landed(ref, sem):
        pltpu.make_async_copy(ref, ref, sem).wait()

    partners = [dev(((z + i) % 8) % 2 * 2 + c, y * 4 + ((z + i) % 8) // 2) for i in range(1, 8)]
    partners += [dev(g, (y + 1) % 4 * 4 + zh), dev(g, (y + 3) % 4 * 4 + zh), dev(sib, s)]
    partners += [dev(g, s, (t + i) % 4) for i in range(1, 4)]
    partners += [dev(i * 2 + c, other) for i in range(2) for other in (s_up, s_down)]
    barrier = pltpu.get_barrier_semaphore()
    for partner in partners:
        pl.semaphore_signal(barrier, inc=1, device_id=partner, device_id_type=MESH)
    pl.semaphore_wait(barrier, len(partners))

    first = ((k_hbm, k_buf.at[g, s]), (q_hbm, q_buf.at[zl, zh]), (v_hbm, v_buf.at[g, s]))

    def first_copy(i, h):
        src = first[i][0].at[:, h * HEAD:(h + 1) * HEAD]
        return remote(
            src, first[i][1], first_send.at[i, h], first_recv.at[i, zl, zh],
            dev(h % 2 * 2 + c, y * 4 + h // 2),
        )

    for i in range(3):
        for h in range(HEADS_TILE):
            @pl.when(z != h)
            def _():
                first_copy(i, h).start()

            @pl.when(z == h)
            def _():
                pltpu.make_async_copy(
                    first[i][0].at[:, h * HEAD:(h + 1) * HEAD], first[i][1], first_recv.at[i, zl, zh]
                ).start()

    loads = [
        pltpu.make_async_copy(src, dst, load_sem.at[i])
        for i, (src, dst) in enumerate(
            ((wb_hbm, wb), (lat_hbm, lat.at[:, 2:6]), (wq_hbm, wq), (wk_hbm, wk), (wv_hbm, wv))
        )
    ]
    for load in loads:
        load.start()
    mine, theirs = pl.ds(2 * c, 2), pl.ds(2 * (1 - c), 2)
    row_copies = [
        remote(lat_hbm.at[mine, 2:4], lat.at[mine, 0:2], row_send.at[0], row_recv.at[0], dev(g, s_up)),
        remote(lat_hbm.at[mine, 0:2], lat.at[mine, 6:8], row_send.at[1], row_recv.at[1], dev(g, s_down)),
    ]
    for copy in row_copies:
        copy.start()

    y_up, y_down, y_far = (y + 1) % 4, (y + 3) % 4, (y + 2) % 4
    bufs = (k_buf, v_buf)

    def region(kind, frame, row):
        return bufs[kind].at[frame, pl.ds(4 * row, 4)]

    def second(kind, frame, row, send, to):
        ref = region(kind, frame, row)
        return remote(ref, ref, send, second_recv.at[kind, frame, row], to)

    def attend(row, core):
        def half(i, carry):
            own = stretch[2 * i + c]
            queries = q_buf[i].reshape(256, HEAD)
            scores, lows = [], []
            for part in range(2):
                frame = 2 * part + core
                keys = k_buf[frame, pl.ds(4 * row, 4)].reshape(256, HEAD)
                scores.append(lax.dot_general(queries, keys, NT, preferred_element_type=F32))
                lows.append(jnp.where(stretch[frame] <= own, 0.0, LOW))
            top = m_ref[i]
            block_top = jnp.maximum(
                jnp.max(scores[0], axis=1, keepdims=True) + lows[0],
                jnp.max(scores[1], axis=1, keepdims=True) + lows[1],
            )
            new_top = jnp.maximum(top, block_top)
            carried = jnp.exp2((top - new_top) * EXP2_SCALE)
            shift = new_top[:, :1] * EXP2_SCALE
            total = l_ref[i] * carried
            blended = acc_ref[i] * carried
            for part in range(2):
                frame = 2 * part + core
                weights = jnp.exp2(scores[part] * EXP2_SCALE - (shift - lows[part]))
                total += weights[:, :HEAD] + weights[:, HEAD:]
                values = v_buf[frame, pl.ds(4 * row, 4)].reshape(256, HEAD)
                blended += dot(weights.astype(BF16), values)
            m_ref[i] = new_top
            l_ref[i] = total
            acc_ref[i] = blended
            return carry

        lax.fori_loop(0, 2, half, 0)

    @pl.when(z < HEADS_TILE)
    def _():
        m_ref[...] = jnp.full_like(m_ref, LOW)
        l_ref[...] = jnp.zeros_like(l_ref)
        acc_ref[...] = jnp.zeros_like(acc_ref)
        pending = []

        def send(copy):
            copy.start()
            pending.append(copy)

        for kind in range(2):
            for i in range(2):
                frame = 2 * i + c
                for j in range(4):
                    landed(bufs[kind].at[frame, 4 * y + j], first_recv.at[2 * kind, i, j])
                send(second(kind, frame, y, own_send.at[kind, i, 0], dev(g, y_up * 4 + zh)))
                send(second(kind, frame, y, own_send.at[kind, i, 1], dev(g, y_down * 4 + zh)))
                send(second(kind, frame, y, own_send.at[kind, i, 2], dev(sib, s)))
            if kind == 0:
                for i in range(2):
                    for j in range(4):
                        landed(q_buf.at[i, j], first_recv.at[1, i, j])

        for step, row in enumerate((y, y_down, y_up, y_far)):
            if step > 0:
                for kind in range(2):
                    for i in range(2):
                        frame = 2 * i + c
                        landed(region(kind, frame, row), second_recv.at[kind, frame, row])
                        if (step, kind) == (1, 0):
                            send(second(kind, frame, row, fwd_send.at[kind, i], dev(g, y_up * 4 + zh)))
                        if (step, kind) == (2, 1):
                            send(second(kind, frame, row, fwd_send.at[kind, i], dev(g, y_down * 4 + zh)))
                        send(second(kind, frame, row, relay_send.at[step - 1, kind, i], dev(sib, s)))
            attend(row, c)
            for kind in range(2):
                for i in range(2):
                    frame = 2 * i + 1 - c
                    landed(region(kind, frame, row), second_recv.at[kind, frame, row])
            attend(row, 1 - c)

        for i in range(2):
            total = jnp.sum(l_ref[i], axis=1, keepdims=True)
            o_buf[i] = (acc_ref[i] / total).astype(BF16).reshape(4, 64, HEAD)

        columns = pl.ds(pl.multiple_of(z * HEAD, HEAD), HEAD)

        def returned(i, j):
            return remote(
                o_buf.at[i, j], a_buf.at[:, columns], ret_send.at[i, j], ret_recv.at[z],
                dev(2 * i + c, y * 4 + j),
            )

        for i in range(2):
            for j in range(4):
                @pl.when(z != 2 * j + i)
                def _():
                    returned(i, j).start()

                @pl.when(z == 2 * j + i)
                def _():
                    pltpu.make_async_copy(o_buf.at[i, j], a_buf.at[:, columns], ret_recv.at[z]).start()
        for copy in pending:
            copy.wait_send()
        for i in range(2):
            for j in range(4):
                @pl.when(z != 2 * j + i)
                def _():
                    returned(i, j).wait_send()

    row_relays = []
    for i, rows in enumerate((slice(0, 2), slice(6, 8))):
        landed(lat.at[mine, rows], row_recv.at[i])
        ref = lat.at[mine, rows]
        row_relays.append(remote(ref, ref, row_send.at[2 + i], row_recv.at[2 + i], dev(sib, s)))
        row_relays[-1].start()

    loads[0].wait()
    for h in range(HEADS_TILE):
        landed(a_buf.at[:, h * HEAD:(h + 1) * HEAD], ret_recv.at[h])
    attended = a_buf[...]
    row_id, token = iota((256, 64), 0), iota((256, 64), 1)
    partial = jnp.zeros((256, 512), F32)
    for part in range(3):
        place = (row_id & 31) - 10 * part
        column = (row_id >> 6) * 8 - 1 + place
        fits = (place >= 0) & (place < 10) & (column >= 0) & (column < 32)
        chosen = one_hot(fits & (((row_id >> 5) & 1) * 32 + column == token))
        rows = dot(chosen, attended).astype(BF16)
        partial += dot(rows, wb[:, 512 * part:512 * (part + 1)])
    p_own[...] = partial.reshape(4, 64, 512)
    p_send[...] = partial.astype(BF16).reshape(4, 64, 512)
    tile_copies = [
        remote(
            p_send.at[(t + i) % 4], p_recv.at[i - 1], tile_send.at[i - 1], tile_recv.at[i - 1],
            dev(g, s, (t + i) % 4),
        )
        for i in range(1, 4)
    ]
    for copy in tile_copies:
        copy.start()

    loads[1].wait()
    for i, rows in enumerate((slice(0, 2), slice(6, 8))):
        landed(lat.at[theirs, rows], row_recv.at[2 + i])
    flat_lat = lat[...].reshape(512, 1536)
    edge_id, cell = iota((64, 512), 0), iota((64, 512), 1)
    col_copies = []
    for i, (start, neighbour) in enumerate(((14, (t + 1) % 4), (0, (t + 3) % 4))):
        chosen = one_hot((edge_id >> 1) * 16 + (edge_id & 1) + start == cell)
        edge_out[i] = dot(chosen, flat_lat).astype(BF16)
        col_copies.append(
            remote(edge_out.at[i], edge_in.at[i], col_send.at[i], col_recv.at[i], dev(g, s, neighbour))
        )
        col_copies[-1].start()

    for i in range(3):
        landed(p_recv.at[i], tile_recv.at[i])
    summed = p_own[t]
    for i in range(3):
        summed += p_recv[i].astype(F32)
    squares = summed * summed
    squares = squares[:, :128] + squares[:, 128:256] + squares[:, 256:384] + squares[:, 384:]
    left, right = iota((64, 64), 0), iota((64, 64), 1)

    def token_of(row):
        place = row & 31
        return place - jnp.where(place >= 10, 10, 0) - jnp.where(place >= 20, 10, 0)

    same = ((left >> 5) == (right >> 5)) & (token_of(left) == token_of(right))
    together = jnp.dot(
        jnp.where(same, 1.0, 0.0), squares, preferred_element_type=F32, precision=lax.Precision.HIGHEST
    )
    mean = jnp.sum(together, axis=1, keepdims=True) * (1.0 / 1536)
    cond[g, 1:3] = (summed * lax.rsqrt(mean + EPS)).astype(BF16).reshape(2, 32, 512)

    slots = (slice(1, 3), slice(0, 1), slice(3, 4))

    def cond_copy(frame, src, slot, sem, to):
        return remote(cond.at[frame, src], cond.at[frame, slots[slot]], cond_send.at[sem], cond_recv.at[frame, slot], to)

    cond_copies = [
        cond_copy(g, slots[0], 0, 0, dev((1 - zl) * 2 + c, s)),
        cond_copy(g, slice(2, 3), 1, 1, dev(c, s_up)),
        cond_copy(g, slice(2, 3), 1, 2, dev(2 + c, s_up)),
        cond_copy(g, slice(1, 2), 2, 3, dev(c, s_down)),
        cond_copy(g, slice(1, 2), 2, 4, dev(2 + c, s_down)),
        cond_copy(g, slots[0], 0, 5, dev(sib, s)),
    ]
    for copy in cond_copies:
        copy.start()
    arrivals = [((1 - zl) * 2 + c, 0), (c, 1), (2 + c, 1), (c, 2), (2 + c, 2)]
    for i, (frame, slot) in enumerate(arrivals):
        landed(cond.at[frame, slots[slot]], cond_recv.at[frame, slot])
        cond_copies.append(cond_copy(frame, slots[slot], slot, 6 + i, dev(sib, s)))
        cond_copies[-1].start()
    for i in range(2):
        landed(edge_in.at[i], col_recv.at[i])
    for load in loads[2:]:
        load.wait()

    cell, source = iota((160, 128), 0), iota((160, 128), 1)
    side = cell - 128
    cell_row = jnp.where(cell < 128, cell >> 4, (side >> 1) & 7)
    cell_token = jnp.where(cell < 128, 1 + ((cell & 15) >> 1), jnp.where(side < 16, 0, 9))
    spread = [one_hot((cell_row >> 1) * 32 + 10 * part + cell_token == source) for part in range(3)]

    query, key = iota((64, 160), 0), iota((64, 160), 1)
    side = key - 128
    key_row = jnp.where(key < 128, key >> 4, (side >> 1) & 7)
    key_col = jnp.where(key < 128, 2 + (key & 15), (side & 1) + jnp.where(side < 16, 0, 18))
    row_off, col_off = key_row - (query >> 4) - 2, key_col - (query & 15) - 2
    row_at, col_at = 4 * s - 2 + key_row, 16 * t - 2 + key_col
    near = (jnp.abs(row_off) <= 2) & (jnp.abs(col_off) <= 2)
    near = near & (row_at >= 0) & (row_at < 64) & (col_at >= 0) & (col_at < 64)
    low = jnp.where(near, 0.0, LOW)

    def layer(core):
        def norm(i, carry):
            frame = 2 * i + core
            rows = pl.ds(pl.multiple_of(frame * 16, 16), 16)
            token_rows = cond[frame].reshape(128, 512)
            hidden, square = [], 0.0
            for part in range(3):
                lanes = slice(512 * part, 512 * (part + 1))
                cells = jnp.concatenate(
                    [lat[frame, :, :, lanes].reshape(128, 512), edge_in[0, rows, lanes], edge_in[1, rows, lanes]], axis=0
                ).astype(F32)
                cells = cells + dot(spread[part], token_rows)
                hidden.append(cells)
                square = square + jnp.sum(cells * cells, axis=1, keepdims=True)
            scale = lax.rsqrt(square * (1.0 / 1536) + EPS)
            for part in range(3):
                x_buf[i, :, 512 * part:512 * (part + 1)] = (hidden[part] * scale).astype(BF16)
            return carry

        lax.fori_loop(0, 2, norm, 0)
        cells = x_buf[...].reshape(320, 1536)
        sr_k[...] = dot(cells, wk[...]).astype(BF16).reshape(2, 160, 384)
        sr_v[...] = dot(cells, wv[...]).astype(BF16).reshape(2, 160, 384)
        sr_q[...] = dot(x_buf[:, 32:96].reshape(128, 1536), wq[...]).astype(BF16).reshape(2, 64, 384)

        def near_attention(i, carry):
            for h in range(3):
                lanes = slice(h * HEAD, (h + 1) * HEAD)
                scores = lax.dot_general(
                    sr_q[i, :, lanes], sr_k[i, :, lanes], NT, preferred_element_type=F32
                )
                scores = scores * HEAD ** (-0.5) + low
                unscaled = jnp.exp(scores - jnp.max(scores, axis=1, keepdims=True))
                weights = (unscaled / jnp.sum(unscaled, axis=1, keepdims=True)).astype(BF16)
                blended = dot(weights, sr_v[i, :, lanes]).astype(BF16)
                out_buf[2 * i + core, :, :, lanes] = blended.reshape(4, 16, HEAD)
            return carry

        lax.fori_loop(0, 2, near_attention, 0)

    layer(c)
    for frame, slot in [(sib, 0)] + [(2 * i + 1 - c, slot) for i, slot in ((0, 1), (1, 1), (0, 2), (1, 2))] + [((1 - zl) * 2 + 1 - c, 0)]:
        landed(cond.at[frame, slots[slot]], cond_recv.at[frame, slot])
    layer(1 - c)
    result = pltpu.make_async_copy(out_buf, out_hbm, out_sem)
    result.start()

    for i in range(3):
        for h in range(HEADS_TILE):
            @pl.when(z != h)
            def _():
                first_copy(i, h).wait_send()
    for copy in row_copies + row_relays + tile_copies + col_copies + cond_copies:
        copy.wait_send()
    result.wait()


def local(base_q, base_k, base_v, frame_stretch, bridge_w, sr_latent, sr_wq, sr_wk, sr_wv):
    hbm = pl.BlockSpec(memory_space=pl.ANY)
    dma = pltpu.SemaphoreType.DMA
    vmem = pltpu.VMEM
    call = pl.pallas_call(
        kernel,
        out_shape=jax.ShapeDtypeStruct((4, 4, 16, 384), BF16),
        in_specs=[hbm, hbm, hbm, pl.BlockSpec(memory_space=pltpu.SMEM)] + [hbm] * 5,
        out_specs=hbm,
        scratch_shapes=[
            vmem((2, 4, 64, HEAD), BF16),
            vmem((4, 16, 64, HEAD), BF16),
            vmem((4, 16, 64, HEAD), BF16),
            vmem((2, 256, HEAD), F32),
            vmem((2, 256, HEAD), F32),
            vmem((2, 256, HEAD), F32),
            vmem((2, 4, 64, HEAD), BF16),
            vmem((64, 768), BF16),
            vmem((768, 1536), BF16),
            vmem((1536, 384), BF16),
            vmem((1536, 384), BF16),
            vmem((1536, 384), BF16),
            vmem((4, 8, 16, 1536), BF16),
            vmem((2, 64, 1536), BF16),
            vmem((2, 64, 1536), BF16),
            vmem((4, 64, 512), F32),
            vmem((4, 64, 512), BF16),
            vmem((3, 64, 512), BF16),
            vmem((4, 4, 32, 512), BF16),
            vmem((2, 160, 1536), BF16),
            vmem((2, 64, 384), BF16),
            vmem((2, 160, 384), BF16),
            vmem((2, 160, 384), BF16),
            vmem((4, 4, 16, 384), BF16),
            dma((3, HEADS_TILE)),
            dma((3, 2, 4)),
            dma((2, 2, 3)),
            dma((2, 2)),
            dma((3, 2, 2)),
            dma((2, 4, 4)),
            dma((2, 4)),
            dma((HEADS_TILE,)),
            dma((3,)),
            dma((3,)),
            dma((11,)),
            dma((4, 3)),
            dma((4,)),
            dma((4,)),
            dma((2,)),
            dma((2,)),
            dma((5,)),
            dma,
        ],
        compiler_params=pltpu.CompilerParams(
            collective_id=0, has_side_effects=True, vmem_limit_bytes=50 * 1024 * 1024
        ),
        cost_estimate=pl.CostEstimate(flops=4 * 10**9, bytes_accessed=16 * 2**20, transcendentals=2 * 10**6),
    )
    return call(
        base_q.reshape(64, 768), base_k.reshape(64, 768), base_v.reshape(64, 768), frame_stretch,
        bridge_w, sr_latent, sr_wq, sr_wk, sr_wv,
    )


def solution(mesh):
    placed = (
        P("grp", "seq", None, "tile"),
        P("grp", "seq", None, "tile"),
        P("grp", "seq", None, "tile"),
        P(),
        P("tile", None),
        P(None, "seq", "tile", None),
        P(None, "grp"),
        P(None, "grp"),
        P(None, "grp"),
    )
    return jax.shard_map(
        local, mesh=mesh, in_specs=placed, out_specs=P(None, "seq", "tile", "grp"), check_vma=False
    )
```

time: 617 us -> 74.5 us (0.12)
  the two profiles are of different devices: /device:TPU:6 before, /device:TPU:32 now
where the time goes in v1:
time: 74.5 us; the launch traced here: 74.2 us
  Pallas kernels  66.5 us (89%)
  local copies, waits for them, and re-layouts  7.68 us (10%)
    pallas_call x1, Pallas kernels, local(): call(base_q.reshape(64, 768), base_k.reshape(64, 768), base_v.reshape(64,...  66.5 us
    unnamed x15, local copies, waits for them, and re-layouts  7.68 us

profile of v1, /device:TPU:32, one launch (start us, length us, event | category | flops | bytes accessed | tf_op | source)
XLA Modules:
  0.0 74.2 jit_solution(13005223563623259516)
XLA Ops:
  0.0 0.0 copy-start
  0.0 1.3 %copy-done = bf16[1536,384]{1,0:T(8,128)(2,1)S(1)} copy-done((bf16[1536,384]{1,0:T(8,128)(2,1)S(1)}, bf16[1536,384]{1,0:T(8,128)(2,1)}, u32[]{:S(2)}) %copy-start) | copy-done | bytes 1179672
  1.3 0.0 copy-start.1
  1.3 1.3 %copy-done.1 = bf16[1536,384]{1,0:T(8,128)(2,1)S(1)} copy-done((bf16[1536,384]{1,0:T(8,128)(2,1)S(1)}, bf16[1536,384]{1,0:T(8,128)(2,1)}, u32[]{:S(2)}) %copy-start.1) | copy-done | bytes 1179672
  2.5 0.0 copy-start.2
  2.5 1.1 %copy-done.2 = bf16[4,4,16,1536]{3,2,1,0:T(8,128)(2,1)S(1)} copy-done((bf16[4,4,16,1536]{3,2,1,0:T(8,128)(2,1)S(1)}, bf16[4,4,16,1536]{3,2,1,0:T(8,128)(2,1)}, u32[]{:S(2)}) %copy-start.2) | copy-done | bytes 786456
  3.7 0.0 copy-start.3
  3.7 0.9 %copy-done.3 = bf16[1,2,32,768]{3,2,1,0:T(8,128)(2,1)S(1)} copy-done((bf16[1,2,32,768]{3,2,1,0:T(8,128)(2,1)S(1)}, bf16[1,2,32,768]{3,2,1,0:T(8,128)(2,1)}, u32[]{:S(2)}) %copy-start.3) | copy-done | bytes 98328
  4.6 0.0 copy-start.4
  4.6 0.9 %copy-done.4 = bf16[1,2,32,768]{3,2,1,0:T(8,128)(2,1)S(1)} copy-done((bf16[1,2,32,768]{3,2,1,0:T(8,128)(2,1)S(1)}, bf16[1,2,32,768]{3,2,1,0:T(8,128)(2,1)}, u32[]{:S(2)}) %copy-start.4) | copy-done | bytes 98328
  5.5 0.0 copy-start.5
  5.5 0.9 %copy-done.5 = bf16[1,2,32,768]{3,2,1,0:T(8,128)(2,1)S(1)} copy-done((bf16[1,2,32,768]{3,2,1,0:T(8,128)(2,1)S(1)}, bf16[1,2,32,768]{3,2,1,0:T(8,128)(2,1)}, u32[]{:S(2)}) %copy-start.5) | copy-done | bytes 98328
  6.4 0.0 copy-start.6
  6.4 0.7 copy-done.6
  7.0 66.5 %shard_map.91 = bf16[4,4,16,384]{3,2,1,0:T(8,128)(2,1)S(1)} custom-call(bf16[64,768]{1,0:T(8,128)(2,1)S(1)} %bitcast.3, bf16[64,768]{1,0:T(8,128)(2,1)S(1)} %bitcast.4, bf16[64,768]{1,0:T(8,128)(2,1)S(1)} %bitcast.5, s32[4]{0:T(128)S(1)} %copy-done.6, bf16[768,1536]{1,0:T(8,128)(2,1)} %wb_hbm.1, bf16[4,4,16,1536]{3,2,1,0:T(8,128)(2,1)S(1)} %copy-done.2, ...), custom_call_target="tpu_custom_call" | custom-call | flops 4000000000 | bytes 16777216 | tf_op jit(solution)/shard_map/pallas_call | solution.py:442
  73.5 0.7 copy.11
Async XLA Ops:
  0.0 1.3 %copy-start = (bf16[1536,384]{1,0:T(8,128)(2,1)S(1)}, bf16[1536,384]{1,0:T(8,128)(2,1)}, u32[]{:S(2)}) copy-start(bf16[1536,384]{1,0:T(8,128)(2,1)} %wq_hbm.1) | copy-start | bytes 3538948
  1.3 1.3 %copy-start.1 = (bf16[1536,384]{1,0:T(8,128)(2,1)S(1)}, bf16[1536,384]{1,0:T(8,128)(2,1)}, u32[]{:S(2)}) copy-start(bf16[1536,384]{1,0:T(8,128)(2,1)} %wk_hbm.1) | copy-start | bytes 3538948
  2.5 1.1 %copy-start.2 = (bf16[4,4,16,1536]{3,2,1,0:T(8,128)(2,1)S(1)}, bf16[4,4,16,1536]{3,2,1,0:T(8,128)(2,1)}, u32[]{:S(2)}) copy-start(bf16[4,4,16,1536]{3,2,1,0:T(8,128)(2,1)} %lat_hbm.1) | copy-start | bytes 2359300
  3.7 0.9 %copy-start.3 = (bf16[1,2,32,768]{3,2,1,0:T(8,128)(2,1)S(1)}, bf16[1,2,32,768]{3,2,1,0:T(8,128)(2,1)}, u32[]{:S(2)}) copy-start(bf16[1,2,32,768]{3,2,1,0:T(8,128)(2,1)} %param.9) | copy-start | bytes 294916
  4.6 0.9 %copy-start.4 = (bf16[1,2,32,768]{3,2,1,0:T(8,128)(2,1)S(1)}, bf16[1,2,32,768]{3,2,1,0:T(8,128)(2,1)}, u32[]{:S(2)}) copy-start(bf16[1,2,32,768]{3,2,1,0:T(8,128)(2,1)} %param.10) | copy-start | bytes 294916
  5.5 0.9 %copy-start.5 = (bf16[1,2,32,768]{3,2,1,0:T(8,128)(2,1)S(1)}, bf16[1,2,32,768]{3,2,1,0:T(8,128)(2,1)}, u32[]{:S(2)}) copy-start(bf16[1,2,32,768]{3,2,1,0:T(8,128)(2,1)} %param.11) | copy-start | bytes 294916
  6.4 0.7 copy-start.6

commit v2 on v1

--- a/solution.py
+++ b/solution.py
@@ -32,12 +32,12 @@
 
 
 def kernel(
-    q_hbm, k_hbm, v_hbm, stretch, wb_hbm, lat_hbm, wq_hbm, wk_hbm, wv_hbm, out_hbm,
-    q_buf, k_buf, v_buf, m_ref, l_ref, acc_ref, o_buf, a_buf, wb, wq, wk, wv,
-    lat, edge_out, edge_in, p_own, p_send, p_recv, cond, x_buf, sr_q, sr_k, sr_v, out_buf,
+    q_hbm, k_hbm, v_hbm, stretch_hbm, wb_hbm, lat_hbm, wq_hbm, wk_hbm, wv_hbm, out_hbm,
+    stretch, q_buf, k_buf, v_buf, m_ref, l_ref, acc_ref, o_buf, a_buf, wb, wq, wk, wv,
+    lat, lat_sq, lat_q, lat_k, lat_v, edge_out, p_own, p_send, p_recv, cond, tok, out_buf,
     first_send, first_recv, own_send, fwd_send, relay_send, second_recv, ret_send, ret_recv,
     tile_send, tile_recv, cond_send, cond_recv, row_send, row_recv, col_send, col_recv,
-    load_sem, out_sem,
+    load_sem, out_sem, near_sem,
 ):
     g, s, t = (lax.axis_index(name) for name in ("grp", "seq", "tile"))
     zl, c = g // 2, g % 2
@@ -60,13 +60,12 @@
     partners = [dev(((z + i) % 8) % 2 * 2 + c, y * 4 + ((z + i) % 8) // 2) for i in range(1, 8)]
     partners += [dev(g, (y + 1) % 4 * 4 + zh), dev(g, (y + 3) % 4 * 4 + zh), dev(sib, s)]
     partners += [dev(g, s, (t + i) % 4) for i in range(1, 4)]
-    partners += [dev(i * 2 + c, other) for i in range(2) for other in (s_up, s_down)]
     barrier = pltpu.get_barrier_semaphore()
     for partner in partners:
         pl.semaphore_signal(barrier, inc=1, device_id=partner, device_id_type=MESH)
     pl.semaphore_wait(barrier, len(partners))
 
-    first = ((k_hbm, k_buf.at[g, s]), (q_hbm, q_buf.at[zl, zh]), (v_hbm, v_buf.at[g, s]))
+    first = ((k_hbm, k_buf.at[g, s]), (v_hbm, v_buf.at[g, s]), (q_hbm, q_buf.at[zl, zh]))
 
     def first_copy(i, h):
         src = first[i][0].at[:, h * HEAD:(h + 1) * HEAD]
@@ -89,21 +88,43 @@
 
     loads = [
         pltpu.make_async_copy(src, dst, load_sem.at[i])
-        for i, (src, dst) in enumerate(
-            ((wb_hbm, wb), (lat_hbm, lat.at[:, 2:6]), (wq_hbm, wq), (wk_hbm, wk), (wv_hbm, wv))
-        )
+        for i, (src, dst) in enumerate((
+            (stretch_hbm, stretch), (lat_hbm, lat.at[:, 32:96]), (wk_hbm, wk), (wv_hbm, wv), (wq_hbm, wq), (wb_hbm, wb),
+        ))
     ]
     for load in loads:
         load.start()
+
+    y_up, y_down, y_far = (y + 1) % 4, (y + 3) % 4, (y + 2) % 4
+    for other in (y_up, y_down):
+        pl.semaphore_signal(near_sem, inc=1, device_id=dev(g, other * 4 + zh), device_id_type=MESH)
+    pl.semaphore_wait(near_sem, 2)
+
     mine, theirs = pl.ds(2 * c, 2), pl.ds(2 * (1 - c), 2)
     row_copies = [
-        remote(lat_hbm.at[mine, 2:4], lat.at[mine, 0:2], row_send.at[0], row_recv.at[0], dev(g, s_up)),
-        remote(lat_hbm.at[mine, 0:2], lat.at[mine, 6:8], row_send.at[1], row_recv.at[1], dev(g, s_down)),
+        remote(lat_hbm.at[mine, 32:64], lat.at[mine, 0:32], row_send.at[0], row_recv.at[0], dev(g, s_up)),
+        remote(lat_hbm.at[mine, 0:32], lat.at[mine, 96:128], row_send.at[1], row_recv.at[1], dev(g, s_down)),
     ]
     for copy in row_copies:
         copy.start()
 
-    y_up, y_down, y_far = (y + 1) % 4, (y + 3) % 4, (y + 2) % 4
+    def project(refs, rows):
+        count = rows.stop - rows.start
+        cells = lat[:, rows].reshape(4 * count, 1536)
+        for weight, ref in refs:
+            ref[:, rows] = dot(cells, weight[...]).reshape(4, count, 384)
+        wide = cells.astype(F32)
+        squares = wide[:, :HEAD] * wide[:, :HEAD]
+        for i in range(1, 12):
+            lanes = slice(HEAD * i, HEAD * (i + 1))
+            squares += wide[:, lanes] * wide[:, lanes]
+        lat_sq[:, rows] = squares.reshape(4, count, HEAD)
+
+    for load in loads[:5]:
+        load.wait()
+    project(((wk, lat_k), (wv, lat_v)), slice(32, 96))
+    lat_q[...] = dot(lat[:, 32:96].reshape(256, 1536), wq[...]).reshape(4, 64, 384)
+
     bufs = (k_buf, v_buf)
 
     def region(kind, frame, row):
@@ -144,7 +165,8 @@
             acc_ref[i] = blended
             return carry
 
-        lax.fori_loop(0, 2, half, 0)
+        for i in range(2):
+            half(i, 0)
 
     @pl.when(z < HEADS_TILE)
     def _():
@@ -161,42 +183,56 @@
             for i in range(2):
                 frame = 2 * i + c
                 for j in range(4):
-                    landed(bufs[kind].at[frame, 4 * y + j], first_recv.at[2 * kind, i, j])
+                    landed(bufs[kind].at[frame, 4 * y + j], first_recv.at[kind, i, j])
                 send(second(kind, frame, y, own_send.at[kind, i, 0], dev(g, y_up * 4 + zh)))
                 send(second(kind, frame, y, own_send.at[kind, i, 1], dev(g, y_down * 4 + zh)))
                 send(second(kind, frame, y, own_send.at[kind, i, 2], dev(sib, s)))
-            if kind == 0:
-                for i in range(2):
-                    for j in range(4):
-                        landed(q_buf.at[i, j], first_recv.at[1, i, j])
-
-        for step, row in enumerate((y, y_down, y_up, y_far)):
-            if step > 0:
-                for kind in range(2):
-                    for i in range(2):
-                        frame = 2 * i + c
-                        landed(region(kind, frame, row), second_recv.at[kind, frame, row])
-                        if (step, kind) == (1, 0):
-                            send(second(kind, frame, row, fwd_send.at[kind, i], dev(g, y_up * 4 + zh)))
-                        if (step, kind) == (2, 1):
-                            send(second(kind, frame, row, fwd_send.at[kind, i], dev(g, y_down * 4 + zh)))
-                        send(second(kind, frame, row, relay_send.at[step - 1, kind, i], dev(sib, s)))
-            attend(row, c)
+        for i in range(2):
+            for j in range(4):
+                landed(q_buf.at[i, j], first_recv.at[2, i, j])
+
+        def relay(step, row, kind):
+            for i in range(2):
+                frame = 2 * i + c
+                landed(region(kind, frame, row), second_recv.at[kind, frame, row])
+                if step == 0 and i == 0:
+                    send(second(kind, frame, row, fwd_send.at[kind, i], dev(g, y_up * 4 + zh)))
+                if step == 1 and i == 1:
+                    send(second(kind, frame, row, fwd_send.at[kind, i], dev(g, y_down * 4 + zh)))
+                send(second(kind, frame, row, relay_send.at[step, kind, i], dev(sib, s)))
+
+        def from_sibling(row):
             for kind in range(2):
                 for i in range(2):
                     frame = 2 * i + 1 - c
                     landed(region(kind, frame, row), second_recv.at[kind, frame, row])
-            attend(row, 1 - c)
+
+        attend(y, c)
+        relay(0, y_down, 0)
+        relay(1, y_up, 0)
+        from_sibling(y)
+        attend(y, 1 - c)
+        relay(0, y_down, 1)
+        relay(1, y_up, 1)
+        attend(y_down, c)
+        attend(y_up, c)
+        from_sibling(y_down)
+        attend(y_down, 1 - c)
+        relay(2, y_far, 0)
+        from_sibling(y_up)
+        attend(y_up, 1 - c)
+        relay(2, y_far, 1)
+        attend(y_far, c)
+        from_sibling(y_far)
+        attend(y_far, 1 - c)
 
         for i in range(2):
             total = jnp.sum(l_ref[i], axis=1, keepdims=True)
             o_buf[i] = (acc_ref[i] / total).astype(BF16).reshape(4, 64, HEAD)
 
-        columns = pl.ds(pl.multiple_of(z * HEAD, HEAD), HEAD)
-
         def returned(i, j):
             return remote(
-                o_buf.at[i, j], a_buf.at[:, columns], ret_send.at[i, j], ret_recv.at[z],
+                o_buf.at[i, j], a_buf.at[z], ret_send.at[i, j], ret_recv.at[z],
                 dev(2 * i + c, y * 4 + j),
             )
 
@@ -208,7 +244,7 @@
 
                 @pl.when(z == 2 * j + i)
                 def _():
-                    pltpu.make_async_copy(o_buf.at[i, j], a_buf.at[:, columns], ret_recv.at[z]).start()
+                    pltpu.make_async_copy(o_buf.at[i, j], a_buf.at[z], ret_recv.at[z]).start()
         for copy in pending:
             copy.wait_send()
         for i in range(2):
@@ -218,16 +254,16 @@
                     returned(i, j).wait_send()
 
     row_relays = []
-    for i, rows in enumerate((slice(0, 2), slice(6, 8))):
+    for i, rows in enumerate((slice(0, 32), slice(96, 128))):
         landed(lat.at[mine, rows], row_recv.at[i])
         ref = lat.at[mine, rows]
         row_relays.append(remote(ref, ref, row_send.at[2 + i], row_recv.at[2 + i], dev(sib, s)))
         row_relays[-1].start()
 
-    loads[0].wait()
+    loads[5].wait()
     for h in range(HEADS_TILE):
-        landed(a_buf.at[:, h * HEAD:(h + 1) * HEAD], ret_recv.at[h])
-    attended = a_buf[...]
+        landed(a_buf.at[h], ret_recv.at[h])
+    attended = jnp.concatenate([a_buf[h] for h in range(HEADS_TILE)], axis=1)
     row_id, token = iota((256, 64), 0), iota((256, 64), 1)
     partial = jnp.zeros((256, 512), F32)
     for part in range(3):
@@ -249,19 +285,23 @@
     for copy in tile_copies:
         copy.start()
 
-    loads[1].wait()
-    for i, rows in enumerate((slice(0, 2), slice(6, 8))):
+    for i, rows in enumerate((slice(0, 32), slice(96, 128))):
         landed(lat.at[theirs, rows], row_recv.at[2 + i])
-    flat_lat = lat[...].reshape(512, 1536)
-    edge_id, cell = iota((64, 512), 0), iota((64, 512), 1)
-    col_copies = []
-    for i, (start, neighbour) in enumerate(((14, (t + 1) % 4), (0, (t + 3) % 4))):
-        chosen = one_hot((edge_id >> 1) * 16 + (edge_id & 1) + start == cell)
-        edge_out[i] = dot(chosen, flat_lat).astype(BF16)
-        col_copies.append(
-            remote(edge_out.at[i], edge_in.at[i], col_send.at[i], col_recv.at[i], dev(g, s, neighbour))
-        )
-        col_copies[-1].start()
+    edge_id, cell = iota((32, 128), 0), iota((32, 128), 1)
+    edge_cell = ((edge_id >> 1) & 7) * 16 + (edge_id & 1) + jnp.where(edge_id < 16, 14, 0)
+    chosen = one_hot(edge_cell == cell)
+    for frame in range(4):
+        edges = dot(chosen, lat[frame, 0:128]).astype(BF16)
+        edge_out[0, frame], edge_out[1, frame] = edges[:16], edges[16:]
+    sides = (slice(128, 144), slice(144, 160))
+    col_copies = [
+        remote(edge_out.at[i], lat.at[:, sides[i]], col_send.at[i], col_recv.at[i], dev(g, s, neighbour))
+        for i, neighbour in enumerate(((t + 1) % 4, (t + 3) % 4))
+    ]
+    for copy in col_copies:
+        copy.start()
+    for rows in (slice(0, 32), slice(96, 128)):
+        project(((wk, lat_k), (wv, lat_v)), rows)
 
     for i in range(3):
         landed(p_recv.at[i], tile_recv.at[i])
@@ -298,21 +338,26 @@
     ]
     for copy in cond_copies:
         copy.start()
+    for i in range(2):
+        landed(lat.at[:, sides[i]], col_recv.at[i])
+    project(((wk, lat_k), (wv, lat_v)), slice(128, 160))
     arrivals = [((1 - zl) * 2 + c, 0), (c, 1), (2 + c, 1), (c, 2), (2 + c, 2)]
     for i, (frame, slot) in enumerate(arrivals):
         landed(cond.at[frame, slots[slot]], cond_recv.at[frame, slot])
         cond_copies.append(cond_copy(frame, slots[slot], slot, 6 + i, dev(sib, s)))
         cond_copies[-1].start()
-    for i in range(2):
-        landed(edge_in.at[i], col_recv.at[i])
-    for load in loads[2:]:
-        load.wait()
-
-    cell, source = iota((160, 128), 0), iota((160, 128), 1)
+
+    place, source = iota((64, 128), 0), iota((64, 128), 1)
+    unpack = [
+        one_hot(((place & 15) < 10) & ((place >> 4) * 32 + 10 * part + (place & 15) == source)) for part in range(3)
+    ]
+    cell, source = iota((160, 64), 0), iota((160, 64), 1)
     side = cell - 128
     cell_row = jnp.where(cell < 128, cell >> 4, (side >> 1) & 7)
     cell_token = jnp.where(cell < 128, 1 + ((cell & 15) >> 1), jnp.where(side < 16, 0, 9))
-    spread = [one_hot((cell_row >> 1) * 32 + 10 * part + cell_token == source) for part in range(3)]
+    above = (cell_row >> 1) * 16 + cell_token == source
+    spread = one_hot(above)
+    diagonal = iota((64, 64), 0) == iota((64, 64), 1)
 
     query, key = iota((64, 160), 0), iota((64, 160), 1)
     side = key - 128
@@ -325,44 +370,34 @@
     low = jnp.where(near, 0.0, LOW)
 
     def layer(core):
-        def norm(i, carry):
+        for i in range(2):
+            rows = cond[2 * i + core].reshape(128, 512)
+            for part in range(3):
+                tok[i, :, 512 * part:512 * (part + 1)] = dot(unpack[part], rows).astype(BF16)
+        tokens = tok[...].reshape(128, 1536)
+        parts = [dot(tokens, weight[...]).astype(BF16) for weight in (wk, wv, wq)]
+        for i in range(2):
             frame = 2 * i + core
-            rows = pl.ds(pl.multiple_of(frame * 16, 16), 16)
-            token_rows = cond[frame].reshape(128, 512)
-            hidden, square = [], 0.0
-            for part in range(3):
-                lanes = slice(512 * part, 512 * (part + 1))
-                cells = jnp.concatenate(
-                    [lat[frame, :, :, lanes].reshape(128, 512), edge_in[0, rows, lanes], edge_in[1, rows, lanes]], axis=0
-                ).astype(F32)
-                cells = cells + dot(spread[part], token_rows)
-                hidden.append(cells)
-                square = square + jnp.sum(cells * cells, axis=1, keepdims=True)
+            pair = lax.dot_general(tok[i], tok[i], NT, preferred_element_type=F32)
+            token_sq = jnp.sum(jnp.where(diagonal, pair, 0.0), axis=0, keepdims=True)
+            cross = lax.dot_general(lat[frame], tok[i], NT, preferred_element_type=F32)
+            square = jnp.sum(jnp.where(above, 2.0 * cross + token_sq, 0.0), axis=1, keepdims=True)
+            square = jnp.maximum(square + jnp.sum(lat_sq[frame], axis=1, keepdims=True), 0.0)
             scale = lax.rsqrt(square * (1.0 / 1536) + EPS)
-            for part in range(3):
-                x_buf[i, :, 512 * part:512 * (part + 1)] = (hidden[part] * scale).astype(BF16)
-            return carry
-
-        lax.fori_loop(0, 2, norm, 0)
-        cells = x_buf[...].reshape(320, 1536)
-        sr_k[...] = dot(cells, wk[...]).astype(BF16).reshape(2, 160, 384)
-        sr_v[...] = dot(cells, wv[...]).astype(BF16).reshape(2, 160, 384)
-        sr_q[...] = dot(x_buf[:, 32:96].reshape(128, 1536), wq[...]).astype(BF16).reshape(2, 64, 384)
-
-        def near_attention(i, carry):
+            keys, values = (
+                (scale * (ref[frame] + dot(spread, part[64 * i:64 * (i + 1)]))).astype(BF16)
+                for ref, part in ((lat_k, parts[0]), (lat_v, parts[1]))
+            )
+            queries = dot(spread[32:96], parts[2][64 * i:64 * (i + 1)])
+            queries = (scale[32:96] * (lat_q[frame] + queries)).astype(BF16)
             for h in range(3):
                 lanes = slice(h * HEAD, (h + 1) * HEAD)
-                scores = lax.dot_general(
-                    sr_q[i, :, lanes], sr_k[i, :, lanes], NT, preferred_element_type=F32
-                )
+                scores = lax.dot_general(queries[:, lanes], keys[:, lanes], NT, preferred_element_type=F32)
                 scores = scores * HEAD ** (-0.5) + low
                 unscaled = jnp.exp(scores - jnp.max(scores, axis=1, keepdims=True))
                 weights = (unscaled / jnp.sum(unscaled, axis=1, keepdims=True)).astype(BF16)
-                blended = dot(weights, sr_v[i, :, lanes]).astype(BF16)
-                out_buf[2 * i + core, :, :, lanes] = blended.reshape(4, 16, HEAD)
-            return carry
-
-        lax.fori_loop(0, 2, near_attention, 0)
+                blended = dot(weights, values[:, lanes]).astype(BF16)
+                out_buf[frame, :, :, lanes] = blended.reshape(4, 16, HEAD)
 
     layer(c)
     for frame, slot in [(sib, 0)] + [(2 * i + 1 - c, slot) for i, slot in ((0, 1), (1, 1), (0, 2), (1, 2))] + [((1 - zl) * 2 + 1 - c, 0)]:
@@ -382,15 +417,16 @@
 
 
 def local(base_q, base_k, base_v, frame_stretch, bridge_w, sr_latent, sr_wq, sr_wk, sr_wv):
-    hbm = pl.BlockSpec(memory_space=pl.ANY)
+    hbm = pl.BlockSpec(memory_space=pltpu.HBM)
     dma = pltpu.SemaphoreType.DMA
     vmem = pltpu.VMEM
     call = pl.pallas_call(
         kernel,
         out_shape=jax.ShapeDtypeStruct((4, 4, 16, 384), BF16),
-        in_specs=[hbm, hbm, hbm, pl.BlockSpec(memory_space=pltpu.SMEM)] + [hbm] * 5,
+        in_specs=[hbm] * 9,
         out_specs=hbm,
         scratch_shapes=[
+            pltpu.SMEM((4,), jnp.int32),
             vmem((2, 4, 64, HEAD), BF16),
             vmem((4, 16, 64, HEAD), BF16),
             vmem((4, 16, 64, HEAD), BF16),
@@ -398,22 +434,22 @@
             vmem((2, 256, HEAD), F32),
             vmem((2, 256, HEAD), F32),
             vmem((2, 4, 64, HEAD), BF16),
-            vmem((64, 768), BF16),
+            vmem((HEADS_TILE, 64, HEAD), BF16),
             vmem((768, 1536), BF16),
             vmem((1536, 384), BF16),
             vmem((1536, 384), BF16),
             vmem((1536, 384), BF16),
-            vmem((4, 8, 16, 1536), BF16),
-            vmem((2, 64, 1536), BF16),
-            vmem((2, 64, 1536), BF16),
+            vmem((4, 160, 1536), BF16),
+            vmem((4, 160, HEAD), F32),
+            vmem((4, 64, 384), F32),
+            vmem((4, 160, 384), F32),
+            vmem((4, 160, 384), F32),
+            vmem((2, 4, 16, 1536), BF16),
             vmem((4, 64, 512), F32),
             vmem((4, 64, 512), BF16),
             vmem((3, 64, 512), BF16),
             vmem((4, 4, 32, 512), BF16),
-            vmem((2, 160, 1536), BF16),
-            vmem((2, 64, 384), BF16),
-            vmem((2, 160, 384), BF16),
-            vmem((2, 160, 384), BF16),
+            vmem((2, 64, 1536), BF16),
             vmem((4, 4, 16, 384), BF16),
             dma((3, HEADS_TILE)),
             dma((3, 2, 4)),
@@ -431,17 +467,18 @@
             dma((4,)),
             dma((2,)),
             dma((2,)),
-            dma((5,)),
+            dma((6,)),
             dma,
+            pltpu.SemaphoreType.REGULAR,
         ],
         compiler_params=pltpu.CompilerParams(
-            collective_id=0, has_side_effects=True, vmem_limit_bytes=50 * 1024 * 1024
+            collective_id=0, has_side_effects=True, vmem_limit_bytes=62 * 1024 * 1024
         ),
         cost_estimate=pl.CostEstimate(flops=4 * 10**9, bytes_accessed=16 * 2**20, transcendentals=2 * 10**6),
     )
     return call(
         base_q.reshape(64, 768), base_k.reshape(64, 768), base_v.reshape(64, 768), frame_stretch,
-        bridge_w, sr_latent, sr_wq, sr_wk, sr_wv,
+        bridge_w, sr_latent.reshape(4, 64, 1536), sr_wq, sr_wk, sr_wv,
     )
 
 

time: 74.5 us -> 61 us (0.82)
  Pallas kernels: 66.5 us -> 59.3 us
  local copies, waits for them, and re-layouts: 7.68 us -> 1.62 us
    pallas_call x1, Pallas kernels: 66.5 us -> 59.3 us  [local(): call(base_q.reshape(64, 768), base_k.reshape(64, 768), base_v.reshape(64,...]
    unnamed x15 -> x1, local copies, waits for them, and re-layouts: 7.68 us -> 1.62 us
where the time goes in v2:
time: 61 us; the launch traced here: 60.9 us
  Pallas kernels  59.3 us (97%)
  local copies, waits for them, and re-layouts  1.62 us (3%)
    pallas_call x1, Pallas kernels, local(): call(base_q.reshape(64, 768), base_k.reshape(64, 768), base_v.reshape(64,...  59.3 us
    unnamed x1, local copies, waits for them, and re-layouts  1.62 us

profile of v2, /device:TPU:32, one launch (start us, length us, event | category | flops | bytes accessed | tf_op | source)
XLA Modules:
  0.0 60.9 jit_solution(7505652240503532125)
XLA Ops:
  0.0 59.3 %shard_map.91 = bf16[4,4,16,384]{3,2,1,0:T(8,128)(2,1)} custom-call(bf16[64,768]{1,0:T(8,128)(2,1)} %bitcast.5, bf16[64,768]{1,0:T(8,128)(2,1)} %bitcast.6, bf16[64,768]{1,0:T(8,128)(2,1)} %bitcast.7, s32[4]{0:T(128)} %stretch_hbm.1, bf16[768,1536]{1,0:T(8,128)(2,1)} %wb_hbm.1, bf16[4,64,1536]{2,1,0:T(8,128)(2,1)} %bitcast.4, bf16[1536,384]{1,0:T(8,128)(2,1)} %wq_hbm.1, ...), custom_call_target="tpu_custom_call" | custom-call | flops 4000000000 | bytes 16777216 | tf_op jit(solution)/shard_map/pallas_call | solution.py:479
  59.3 1.6 %copy.11 = bf16[4,4,16,384]{3,2,1,0:T(8,128)(2,1)} copy(bf16[4,4,16,384]{3,2,1,0:T(8,128)(2,1)} %shard_map.91) | data formatting | bytes 393216

commit v3 on v2

--- a/solution.py
+++ b/solution.py
@@ -10,6 +10,7 @@
 
 HEAD = 128
 HEADS_TILE = 6
+PLACE = (0, 1, 2, 3, 4, 5)
 EPS = 1e-06
 LOW = -1e30
 EXP2_SCALE = HEAD ** (-0.5) * math.log2(math.e)
@@ -33,7 +34,7 @@
 
 def kernel(
     q_hbm, k_hbm, v_hbm, stretch_hbm, wb_hbm, lat_hbm, wq_hbm, wk_hbm, wv_hbm, out_hbm,
-    stretch, q_buf, k_buf, v_buf, m_ref, l_ref, acc_ref, o_buf, a_buf, wb, wq, wk, wv,
+    stretch, q_buf, k_buf, v_buf, s_buf, w_buf, m_ref, l_ref, acc_ref, o_buf, a_buf, wb, wq, wk, wv,
     lat, lat_sq, lat_q, lat_k, lat_v, edge_out, p_own, p_send, p_recv, cond, tok, out_buf,
     first_send, first_recv, own_send, fwd_send, relay_send, second_recv, ret_send, ret_recv,
     tile_send, tile_recv, cond_send, cond_recv, row_send, row_recv, col_send, col_recv,
@@ -44,6 +45,7 @@
     y, zh = s // 4, s % 4
     z = zh * 2 + zl
     sib = zl * 2 + (1 - c)
+    head, working = (z + 8 - PLACE[0]) % 8, (z + 8 - PLACE[0]) % 8 < HEADS_TILE
     s_up, s_down = (s + 1) % 16, (s + 15) % 16
 
     def dev(grp, seq, tile=t):
@@ -58,7 +60,7 @@
         pltpu.make_async_copy(ref, ref, sem).wait()
 
     partners = [dev(((z + i) % 8) % 2 * 2 + c, y * 4 + ((z + i) % 8) // 2) for i in range(1, 8)]
-    partners += [dev(g, (y + 1) % 4 * 4 + zh), dev(g, (y + 3) % 4 * 4 + zh), dev(sib, s)]
+    partners += [dev(g, (y + i) % 4 * 4 + zh) for i in (1, 3)] + [dev(sib, s)]
     partners += [dev(g, s, (t + i) % 4) for i in range(1, 4)]
     barrier = pltpu.get_barrier_semaphore()
     for partner in partners:
@@ -71,16 +73,16 @@
         src = first[i][0].at[:, h * HEAD:(h + 1) * HEAD]
         return remote(
             src, first[i][1], first_send.at[i, h], first_recv.at[i, zl, zh],
-            dev(h % 2 * 2 + c, y * 4 + h // 2),
+            dev(PLACE[h] % 2 * 2 + c, y * 4 + PLACE[h] // 2),
         )
 
     for i in range(3):
         for h in range(HEADS_TILE):
-            @pl.when(z != h)
+            @pl.when(z != PLACE[h])
             def _():
                 first_copy(i, h).start()
 
-            @pl.when(z == h)
+            @pl.when(z == PLACE[h])
             def _():
                 pltpu.make_async_copy(
                     first[i][0].at[:, h * HEAD:(h + 1) * HEAD], first[i][1], first_recv.at[i, zl, zh]
@@ -108,17 +110,18 @@
     for copy in row_copies:
         copy.start()
 
-    def project(refs, rows):
-        count = rows.stop - rows.start
-        cells = lat[:, rows].reshape(4 * count, 1536)
-        for weight, ref in refs:
-            ref[:, rows] = dot(cells, weight[...]).reshape(4, count, 384)
+    def project(refs, *pieces):
+        cells = jnp.concatenate([lat[:, rows].reshape(-1, 1536) for rows in pieces], axis=0)
         wide = cells.astype(F32)
         squares = wide[:, :HEAD] * wide[:, :HEAD]
         for i in range(1, 12):
             lanes = slice(HEAD * i, HEAD * (i + 1))
             squares += wide[:, lanes] * wide[:, lanes]
-        lat_sq[:, rows] = squares.reshape(4, count, HEAD)
+        results = [(lat_sq, squares)] + [(ref, dot(cells, weight[...])) for weight, ref in refs]
+        count = cells.shape[0] // len(pieces)
+        for ref, result in results:
+            for i, rows in enumerate(pieces):
+                ref[:, rows] = result[count * i:count * (i + 1)].reshape(4, count // 4, -1)
 
     for load in loads[:5]:
         load.wait()
@@ -134,109 +137,119 @@
         ref = region(kind, frame, row)
         return remote(ref, ref, send, second_recv.at[kind, frame, row], to)
 
-    def attend(row, core):
-        def half(i, carry):
-            own = stretch[2 * i + c]
+    def low_of(i, frame):
+        return jnp.where(stretch[frame] <= stretch[2 * i + c], 0.0, LOW)
+
+    def score(row, core):
+        for i in range(2):
             queries = q_buf[i].reshape(256, HEAD)
-            scores, lows = [], []
+            top = m_ref[i]
             for part in range(2):
                 frame = 2 * part + core
                 keys = k_buf[frame, pl.ds(4 * row, 4)].reshape(256, HEAD)
-                scores.append(lax.dot_general(queries, keys, NT, preferred_element_type=F32))
-                lows.append(jnp.where(stretch[frame] <= own, 0.0, LOW))
-            top = m_ref[i]
-            block_top = jnp.maximum(
-                jnp.max(scores[0], axis=1, keepdims=True) + lows[0],
-                jnp.max(scores[1], axis=1, keepdims=True) + lows[1],
-            )
-            new_top = jnp.maximum(top, block_top)
-            carried = jnp.exp2((top - new_top) * EXP2_SCALE)
-            shift = new_top[:, :1] * EXP2_SCALE
-            total = l_ref[i] * carried
-            blended = acc_ref[i] * carried
+                scores = lax.dot_general(queries, keys, NT, preferred_element_type=F32)
+                s_buf[i, core * 4 + row, :, 256 * part:256 * (part + 1)] = scores
+                top = jnp.maximum(top, jnp.maximum(scores[:, :HEAD], scores[:, HEAD:]) + low_of(i, frame))
+            m_ref[i] = top
+
+    def weigh(i):
+        top = jnp.max(m_ref[i], axis=1, keepdims=True) * EXP2_SCALE
+        m_ref[i] = jnp.broadcast_to(top, (256, HEAD))
+        l_ref[i] = jnp.zeros((256, HEAD), F32)
+
+        def block(j, carry):
+            shift, total = m_ref[i], l_ref[i]
             for part in range(2):
-                frame = 2 * part + core
-                weights = jnp.exp2(scores[part] * EXP2_SCALE - (shift - lows[part]))
-                total += weights[:, :HEAD] + weights[:, HEAD:]
-                values = v_buf[frame, pl.ds(4 * row, 4)].reshape(256, HEAD)
-                blended += dot(weights.astype(BF16), values)
-            m_ref[i] = new_top
+                moved = shift - low_of(i, 2 * part + j // 4)
+                for lane in range(2):
+                    lanes = slice(256 * part + HEAD * lane, 256 * part + HEAD * (lane + 1))
+                    weights = jnp.exp2(s_buf[i, j, :, lanes] * EXP2_SCALE - moved)
+                    total += weights
+                    w_buf[i, j, :, lanes] = weights.astype(BF16)
             l_ref[i] = total
-            acc_ref[i] = blended
             return carry
 
-        for i in range(2):
-            half(i, 0)
-
-    @pl.when(z < HEADS_TILE)
+        lax.fori_loop(0, 8, block, 0)
+
+    def blend(row, core):
+        values = [v_buf[2 * part + core, pl.ds(4 * row, 4)].reshape(256, HEAD) for part in range(2)]
+        values = jnp.concatenate(values, axis=0)
+        for i in range(2):
+            acc_ref[i] += dot(w_buf[i, core * 4 + row], values)
+
+    def returned(i, j):
+        return remote(o_buf.at[i, j], a_buf.at[head], ret_send.at[i, j], ret_recv.at[head], dev(2 * i + c, y * 4 + j))
+
+    own_targets = [dev(g, y_up * 4 + zh), dev(g, y_down * 4 + zh), dev(sib, s)]
+    far_rows = (y_down, y_up, y_far)
+
+    def own_copy(kind, i, j):
+        return second(kind, 2 * i + c, y, own_send.at[kind, i, j], own_targets[j])
+
+    def forward_copy(kind, i):
+        return second(kind, 2 * i + c, far_rows[i], fwd_send.at[kind, i], own_targets[i])
+
+    def relay_copy(kind, i, j):
+        return second(kind, 2 * i + c, far_rows[j], relay_send.at[j, kind, i], dev(sib, s))
+
+    @pl.when(working)
     def _():
         m_ref[...] = jnp.full_like(m_ref, LOW)
-        l_ref[...] = jnp.zeros_like(l_ref)
         acc_ref[...] = jnp.zeros_like(acc_ref)
-        pending = []
-
-        def send(copy):
-            copy.start()
-            pending.append(copy)
 
         for kind in range(2):
             for i in range(2):
-                frame = 2 * i + c
                 for j in range(4):
-                    landed(bufs[kind].at[frame, 4 * y + j], first_recv.at[kind, i, j])
-                send(second(kind, frame, y, own_send.at[kind, i, 0], dev(g, y_up * 4 + zh)))
-                send(second(kind, frame, y, own_send.at[kind, i, 1], dev(g, y_down * 4 + zh)))
-                send(second(kind, frame, y, own_send.at[kind, i, 2], dev(sib, s)))
+                    landed(bufs[kind].at[2 * i + c, 4 * y + j], first_recv.at[kind, i, j])
+                for j in range(3):
+                    own_copy(kind, i, j).start()
         for i in range(2):
             for j in range(4):
                 landed(q_buf.at[i, j], first_recv.at[2, i, j])
 
-        def relay(step, row, kind):
+        def relay(kind, j):
             for i in range(2):
-                frame = 2 * i + c
+                landed(region(kind, 2 * i + c, far_rows[j]), second_recv.at[kind, 2 * i + c, far_rows[j]])
+                if i == j:
+                    forward_copy(kind, i).start()
+                relay_copy(kind, i, j).start()
+
+        def from_sibling(kind, row):
+            for i in range(2):
+                frame = 2 * i + 1 - c
                 landed(region(kind, frame, row), second_recv.at[kind, frame, row])
-                if step == 0 and i == 0:
-                    send(second(kind, frame, row, fwd_send.at[kind, i], dev(g, y_up * 4 + zh)))
-                if step == 1 and i == 1:
-                    send(second(kind, frame, row, fwd_send.at[kind, i], dev(g, y_down * 4 + zh)))
-                send(second(kind, frame, row, relay_send.at[step, kind, i], dev(sib, s)))
-
-        def from_sibling(row):
-            for kind in range(2):
-                for i in range(2):
-                    frame = 2 * i + 1 - c
-                    landed(region(kind, frame, row), second_recv.at[kind, frame, row])
-
-        attend(y, c)
-        relay(0, y_down, 0)
-        relay(1, y_up, 0)
-        from_sibling(y)
-        attend(y, 1 - c)
-        relay(0, y_down, 1)
-        relay(1, y_up, 1)
-        attend(y_down, c)
-        attend(y_up, c)
-        from_sibling(y_down)
-        attend(y_down, 1 - c)
-        relay(2, y_far, 0)
-        from_sibling(y_up)
-        attend(y_up, 1 - c)
-        relay(2, y_far, 1)
-        attend(y_far, c)
-        from_sibling(y_far)
-        attend(y_far, 1 - c)
+
+        score(y, c)
+        for j in range(2):
+            relay(0, j)
+        from_sibling(0, y)
+        score(y, 1 - c)
+        score(y_down, c)
+        score(y_up, c)
+        for j in range(2):
+            relay(1, j)
+        relay(0, 2)
+        for row in (y_down, y_up):
+            from_sibling(0, row)
+            score(row, 1 - c)
+        score(y_far, c)
+        from_sibling(0, y_far)
+        score(y_far, 1 - c)
+        weigh(0)
+        relay(1, 2)
+        weigh(1)
+        blend(y, c)
+        from_sibling(1, y)
+        blend(y, 1 - c)
+        for row in far_rows:
+            blend(row, c)
+        for row in far_rows:
+            from_sibling(1, row)
+            blend(row, 1 - c)
 
         for i in range(2):
             total = jnp.sum(l_ref[i], axis=1, keepdims=True)
             o_buf[i] = (acc_ref[i] / total).astype(BF16).reshape(4, 64, HEAD)
-
-        def returned(i, j):
-            return remote(
-                o_buf.at[i, j], a_buf.at[z], ret_send.at[i, j], ret_recv.at[z],
-                dev(2 * i + c, y * 4 + j),
-            )
-
-        for i in range(2):
             for j in range(4):
                 @pl.when(z != 2 * j + i)
                 def _():
@@ -244,14 +257,7 @@
 
                 @pl.when(z == 2 * j + i)
                 def _():
-                    pltpu.make_async_copy(o_buf.at[i, j], a_buf.at[z], ret_recv.at[z]).start()
-        for copy in pending:
-            copy.wait_send()
-        for i in range(2):
-            for j in range(4):
-                @pl.when(z != 2 * j + i)
-                def _():
-                    returned(i, j).wait_send()
+                    pltpu.make_async_copy(o_buf.at[i, j], a_buf.at[head], ret_recv.at[head]).start()
 
     row_relays = []
     for i, rows in enumerate((slice(0, 32), slice(96, 128))):
@@ -259,6 +265,22 @@
         ref = lat.at[mine, rows]
         row_relays.append(remote(ref, ref, row_send.at[2 + i], row_recv.at[2 + i], dev(sib, s)))
         row_relays[-1].start()
+    for i, rows in enumerate((slice(0, 32), slice(96, 128))):
+        landed(lat.at[theirs, rows], row_recv.at[2 + i])
+    edge_id, cell = iota((32, 128), 0), iota((32, 128), 1)
+    edge_cell = ((edge_id >> 1) & 7) * 16 + (edge_id & 1) + jnp.where(edge_id < 16, 14, 0)
+    chosen = one_hot(edge_cell == cell)
+    for frame in range(4):
+        edges = dot(chosen, lat[frame, 0:128]).astype(BF16)
+        edge_out[0, frame], edge_out[1, frame] = edges[:16], edges[16:]
+    sides = (slice(128, 144), slice(144, 160))
+    col_copies = [
+        remote(edge_out.at[i], lat.at[:, sides[i]], col_send.at[i], col_recv.at[i], dev(g, s, neighbour))
+        for i, neighbour in enumerate(((t + 1) % 4, (t + 3) % 4))
+    ]
+    for copy in col_copies:
+        copy.start()
+    project(((wk, lat_k), (wv, lat_v)), slice(0, 32), slice(96, 128))
 
     loads[5].wait()
     for h in range(HEADS_TILE):
@@ -285,24 +307,6 @@
     for copy in tile_copies:
         copy.start()
 
-    for i, rows in enumerate((slice(0, 32), slice(96, 128))):
-        landed(lat.at[theirs, rows], row_recv.at[2 + i])
-    edge_id, cell = iota((32, 128), 0), iota((32, 128), 1)
-    edge_cell = ((edge_id >> 1) & 7) * 16 + (edge_id & 1) + jnp.where(edge_id < 16, 14, 0)
-    chosen = one_hot(edge_cell == cell)
-    for frame in range(4):
-        edges = dot(chosen, lat[frame, 0:128]).astype(BF16)
-        edge_out[0, frame], edge_out[1, frame] = edges[:16], edges[16:]
-    sides = (slice(128, 144), slice(144, 160))
-    col_copies = [
-        remote(edge_out.at[i], lat.at[:, sides[i]], col_send.at[i], col_recv.at[i], dev(g, s, neighbour))
-        for i, neighbour in enumerate(((t + 1) % 4, (t + 3) % 4))
-    ]
-    for copy in col_copies:
-        copy.start()
-    for rows in (slice(0, 32), slice(96, 128)):
-        project(((wk, lat_k), (wv, lat_v)), rows)
-
     for i in range(3):
         landed(p_recv.at[i], tile_recv.at[i])
     summed = p_own[t]
@@ -328,8 +332,9 @@
     def cond_copy(frame, src, slot, sem, to):
         return remote(cond.at[frame, src], cond.at[frame, slots[slot]], cond_send.at[sem], cond_recv.at[frame, slot], to)
 
+    across = (1 - zl) * 2 + c
     cond_copies = [
-        cond_copy(g, slots[0], 0, 0, dev((1 - zl) * 2 + c, s)),
+        cond_copy(g, slots[0], 0, 0, dev(across, s)),
         cond_copy(g, slice(2, 3), 1, 1, dev(c, s_up)),
         cond_copy(g, slice(2, 3), 1, 2, dev(2 + c, s_up)),
         cond_copy(g, slice(1, 2), 2, 3, dev(c, s_down)),
@@ -376,6 +381,7 @@
                 tok[i, :, 512 * part:512 * (part + 1)] = dot(unpack[part], rows).astype(BF16)
         tokens = tok[...].reshape(128, 1536)
         parts = [dot(tokens, weight[...]).astype(BF16) for weight in (wk, wv, wq)]
+        scores, blocks = [], []
         for i in range(2):
             frame = 2 * i + core
             pair = lax.dot_general(tok[i], tok[i], NT, preferred_element_type=F32)
@@ -392,12 +398,15 @@
             queries = (scale[32:96] * (lat_q[frame] + queries)).astype(BF16)
             for h in range(3):
                 lanes = slice(h * HEAD, (h + 1) * HEAD)
-                scores = lax.dot_general(queries[:, lanes], keys[:, lanes], NT, preferred_element_type=F32)
-                scores = scores * HEAD ** (-0.5) + low
-                unscaled = jnp.exp(scores - jnp.max(scores, axis=1, keepdims=True))
-                weights = (unscaled / jnp.sum(unscaled, axis=1, keepdims=True)).astype(BF16)
-                blended = dot(weights, values[:, lanes]).astype(BF16)
-                out_buf[frame, :, :, lanes] = blended.reshape(4, 16, HEAD)
+                score = lax.dot_general(queries[:, lanes], keys[:, lanes], NT, preferred_element_type=F32)
+                scores.append(score * HEAD ** (-0.5) + low)
+                blocks.append((frame, lanes, values[:, lanes]))
+        scores = jnp.concatenate(scores, axis=0)
+        unscaled = jnp.exp(scores - jnp.max(scores, axis=1, keepdims=True))
+        weights = (unscaled * (1.0 / jnp.sum(unscaled, axis=1, keepdims=True))).astype(BF16)
+        for i, (frame, lanes, values) in enumerate(blocks):
+            blended = dot(weights[64 * i:64 * (i + 1)], values).astype(BF16)
+            out_buf[frame, :, :, lanes] = blended.reshape(4, 16, HEAD)
 
     layer(c)
     for frame, slot in [(sib, 0)] + [(2 * i + 1 - c, slot) for i, slot in ((0, 1), (1, 1), (0, 2), (1, 2))] + [((1 - zl) * 2 + 1 - c, 0)]:
@@ -408,9 +417,23 @@
 
     for i in range(3):
         for h in range(HEADS_TILE):
-            @pl.when(z != h)
+            @pl.when(z != PLACE[h])
             def _():
                 first_copy(i, h).wait_send()
+    @pl.when(working)
+    def _():
+        for kind in range(2):
+            for i in range(2):
+                for j in range(3):
+                    own_copy(kind, i, j).wait_send()
+                    relay_copy(kind, i, j).wait_send()
+                forward_copy(kind, i).wait_send()
+        for i in range(2):
+            for j in range(4):
+                @pl.when(z != 2 * j + i)
+                def _():
+                    returned(i, j).wait_send()
+
     for copy in row_copies + row_relays + tile_copies + col_copies + cond_copies:
         copy.wait_send()
     result.wait()
@@ -430,6 +453,8 @@
             vmem((2, 4, 64, HEAD), BF16),
             vmem((4, 16, 64, HEAD), BF16),
             vmem((4, 16, 64, HEAD), BF16),
+            vmem((2, 8, 256, 512), F32),
+            vmem((2, 8, 256, 512), BF16),
             vmem((2, 256, HEAD), F32),
             vmem((2, 256, HEAD), F32),
             vmem((2, 256, HEAD), F32),

time: 61 us -> 59.1 us (0.969)
  Pallas kernels: 59.3 us -> 57.3 us
    pallas_call x1, Pallas kernels: 59.3 us -> 57.3 us  [local(): call(base_q.reshape(64, 768), base_k.reshape(64, 768), base_v.reshape(64,...]
where the time goes in v3:
time: 59.1 us; the launch traced here: 59 us
  Pallas kernels  57.3 us (97%)
  local copies, waits for them, and re-layouts  1.62 us (3%)
    pallas_call x1, Pallas kernels, local(): call(base_q.reshape(64, 768), base_k.reshape(64, 768), base_v.reshape(64,...  57.3 us
    unnamed x1, local copies, waits for them, and re-layouts  1.62 us

profile of v3, /device:TPU:32, one launch (start us, length us, event | category | flops | bytes accessed | tf_op | source)
XLA Modules:
  0.0 59.0 jit_solution(14708487177824667082)
XLA Ops:
  0.0 57.3 %shard_map.91 = bf16[4,4,16,384]{3,2,1,0:T(8,128)(2,1)} custom-call(bf16[64,768]{1,0:T(8,128)(2,1)} %bitcast.5, bf16[64,768]{1,0:T(8,128)(2,1)} %bitcast.6, bf16[64,768]{1,0:T(8,128)(2,1)} %bitcast.7, s32[4]{0:T(128)} %stretch_hbm.1, bf16[768,1536]{1,0:T(8,128)(2,1)} %wb_hbm.1, bf16[4,64,1536]{2,1,0:T(8,128)(2,1)} %bitcast.4, bf16[1536,384]{1,0:T(8,128)(2,1)} %wq_hbm.1, ...), custom_call_target="tpu_custom_call" | custom-call | flops 4000000000 | bytes 16777216 | tf_op jit(solution)/shard_map/pallas_call | solution.py:504
  57.3 1.6 %copy.11 = bf16[4,4,16,384]{3,2,1,0:T(8,128)(2,1)} copy(bf16[4,4,16,384]{3,2,1,0:T(8,128)(2,1)} %shard_map.91) | data formatting | bytes 393216

commit v4 on v3

--- a/solution.py
+++ b/solution.py
@@ -201,8 +201,9 @@
             for i in range(2):
                 for j in range(4):
                     landed(bufs[kind].at[2 * i + c, 4 * y + j], first_recv.at[kind, i, j])
-                for j in range(3):
-                    own_copy(kind, i, j).start()
+                own_copy(kind, i, i).start()
+            for i, j in ((1, 0), (0, 1), (0, 2), (1, 2)):
+                own_copy(kind, i, j).start()
         for i in range(2):
             for j in range(4):
                 landed(q_buf.at[i, j], first_recv.at[2, i, j])
@@ -236,16 +237,19 @@
         from_sibling(0, y_far)
         score(y_far, 1 - c)
         weigh(0)
-        relay(1, 2)
         weigh(1)
         blend(y, c)
         from_sibling(1, y)
         blend(y, 1 - c)
-        for row in far_rows:
-            blend(row, c)
-        for row in far_rows:
+        blend(y_down, c)
+        blend(y_up, c)
+        relay(1, 2)
+        for row in (y_down, y_up):
             from_sibling(1, row)
             blend(row, 1 - c)
+        blend(y_far, c)
+        from_sibling(1, y_far)
+        blend(y_far, 1 - c)
 
         for i in range(2):
             total = jnp.sum(l_ref[i], axis=1, keepdims=True)
@@ -302,7 +306,7 @@
             p_send.at[(t + i) % 4], p_recv.at[i - 1], tile_send.at[i - 1], tile_recv.at[i - 1],
             dev(g, s, (t + i) % 4),
         )
-        for i in range(1, 4)
+        for i in (2, 1, 3)
     ]
     for copy in tile_copies:
         copy.start()

time: 59.1 us -> 58.3 us (0.986)
  Pallas kernels: 57.3 us -> 56.6 us
    pallas_call x1, Pallas kernels: 57.3 us -> 56.6 us  [local(): call(base_q.reshape(64, 768), base_k.reshape(64, 768), base_v.reshape(64,...]
where the time goes in v4:
time: 58.3 us; the launch traced here: 58.2 us
  Pallas kernels  56.6 us (97%)
  local copies, waits for them, and re-layouts  1.62 us (3%)
    pallas_call x1, Pallas kernels, local(): call(base_q.reshape(64, 768), base_k.reshape(64, 768), base_v.reshape(64,...  56.6 us
    unnamed x1, local copies, waits for them, and re-layouts  1.62 us

profile of v4, /device:TPU:32, one launch (start us, length us, event | category | flops | bytes accessed | tf_op | source)
XLA Modules:
  0.0 58.2 jit_solution(1795213460304254828)
XLA Ops:
  0.0 56.6 %shard_map.91 = bf16[4,4,16,384]{3,2,1,0:T(8,128)(2,1)} custom-call(bf16[64,768]{1,0:T(8,128)(2,1)} %bitcast.5, bf16[64,768]{1,0:T(8,128)(2,1)} %bitcast.6, bf16[64,768]{1,0:T(8,128)(2,1)} %bitcast.7, s32[4]{0:T(128)} %stretch_hbm.1, bf16[768,1536]{1,0:T(8,128)(2,1)} %wb_hbm.1, bf16[4,64,1536]{2,1,0:T(8,128)(2,1)} %bitcast.4, bf16[1536,384]{1,0:T(8,128)(2,1)} %wq_hbm.1, ...), custom_call_target="tpu_custom_call" | custom-call | flops 4000000000 | bytes 16777216 | tf_op jit(solution)/shard_map/pallas_call | solution.py:508
  56.6 1.6 %copy.11 = bf16[4,4,16,384]{3,2,1,0:T(8,128)(2,1)} copy(bf16[4,4,16,384]{3,2,1,0:T(8,128)(2,1)} %shard_map.91) | data formatting | bytes 393216

commit v5 on v4

--- a/solution.py
+++ b/solution.py
@@ -290,30 +290,33 @@
     for h in range(HEADS_TILE):
         landed(a_buf.at[h], ret_recv.at[h])
     attended = jnp.concatenate([a_buf[h] for h in range(HEADS_TILE)], axis=1)
-    row_id, token = iota((256, 64), 0), iota((256, 64), 1)
-    partial = jnp.zeros((256, 512), F32)
-    for part in range(3):
-        place = (row_id & 31) - 10 * part
-        column = (row_id >> 6) * 8 - 1 + place
-        fits = (place >= 0) & (place < 10) & (column >= 0) & (column < 32)
-        chosen = one_hot(fits & (((row_id >> 5) & 1) * 32 + column == token))
-        rows = dot(chosen, attended).astype(BF16)
-        partial += dot(rows, wb[:, 512 * part:512 * (part + 1)])
-    p_own[...] = partial.reshape(4, 64, 512)
-    p_send[...] = partial.astype(BF16).reshape(4, 64, 512)
-    tile_copies = [
-        remote(
-            p_send.at[(t + i) % 4], p_recv.at[i - 1], tile_send.at[i - 1], tile_recv.at[i - 1],
-            dev(g, s, (t + i) % 4),
-        )
-        for i in (2, 1, 3)
-    ]
-    for copy in tile_copies:
-        copy.start()
+    row_id, token = iota((128, 64), 0), iota((128, 64), 1)
+    tile_copies = []
+    for offsets in ((2, 1), (3, 0)):
+        tile = (t + jnp.where(row_id < 64, offsets[0], offsets[1])) & 3
+        partial = jnp.zeros((128, 512), F32)
+        for part in range(3):
+            place = (row_id & 31) - 10 * part
+            column = tile * 8 - 1 + place
+            fits = (place >= 0) & (place < 10) & (column >= 0) & (column < 32)
+            chosen = one_hot(fits & (((row_id >> 5) & 1) * 32 + column == token))
+            rows = dot(chosen, attended).astype(BF16)
+            partial += dot(rows, wb[:, 512 * part:512 * (part + 1)])
+        for i, offset in enumerate(offsets):
+            piece = partial[64 * i:64 * (i + 1)]
+            if offset == 0:
+                p_own[...] = piece
+                continue
+            slot = offset - 1
+            p_send[slot] = piece.astype(BF16)
+            tile_copies.append(remote(
+                p_send.at[slot], p_recv.at[slot], tile_send.at[slot], tile_recv.at[slot], dev(g, s, (t + offset) % 4)
+            ))
+            tile_copies[-1].start()
 
     for i in range(3):
         landed(p_recv.at[i], tile_recv.at[i])
-    summed = p_own[t]
+    summed = p_own[...]
     for i in range(3):
         summed += p_recv[i].astype(F32)
     squares = summed * summed
@@ -474,8 +477,8 @@
             vmem((4, 160, 384), F32),
             vmem((4, 160, 384), F32),
             vmem((2, 4, 16, 1536), BF16),
-            vmem((4, 64, 512), F32),
-            vmem((4, 64, 512), BF16),
+            vmem((64, 512), F32),
+            vmem((3, 64, 512), BF16),
             vmem((3, 64, 512), BF16),
             vmem((4, 4, 32, 512), BF16),
             vmem((2, 64, 1536), BF16),

time: 58.3 us -> 57.9 us (level)
  no operation moved by 1% of the time
where the time goes in v5:
time: 57.9 us; the launch traced here: 57.8 us
  Pallas kernels  56.2 us (97%)
  local copies, waits for them, and re-layouts  1.62 us (3%)
    pallas_call x1, Pallas kernels, local(): call(base_q.reshape(64, 768), base_k.reshape(64, 768), base_v.reshape(64,...  56.2 us
    unnamed x1, local copies, waits for them, and re-layouts  1.62 us

profile of v5, /device:TPU:32, one launch (start us, length us, event | category | flops | bytes accessed | tf_op | source)
XLA Modules:
  0.0 57.8 jit_solution(13703276196465317551)
XLA Ops:
  0.0 56.2 %shard_map.91 = bf16[4,4,16,384]{3,2,1,0:T(8,128)(2,1)} custom-call(bf16[64,768]{1,0:T(8,128)(2,1)} %bitcast.5, bf16[64,768]{1,0:T(8,128)(2,1)} %bitcast.6, bf16[64,768]{1,0:T(8,128)(2,1)} %bitcast.7, s32[4]{0:T(128)} %stretch_hbm.1, bf16[768,1536]{1,0:T(8,128)(2,1)} %wb_hbm.1, bf16[4,64,1536]{2,1,0:T(8,128)(2,1)} %bitcast.4, bf16[1536,384]{1,0:T(8,128)(2,1)} %wq_hbm.1, ...), custom_call_target="tpu_custom_call" | custom-call | flops 4000000000 | bytes 16777216 | tf_op jit(solution)/shard_map/pallas_call | solution.py:511
  56.2 1.6 %copy.11 = bf16[4,4,16,384]{3,2,1,0:T(8,128)(2,1)} copy(bf16[4,4,16,384]{3,2,1,0:T(8,128)(2,1)} %shard_map.91) | data formatting | bytes 393216
